TPU v7x, 128 devices: a whole 4x4x4 slice. The times are simulated.
128 devices in a mesh: blk: 16 (over z, y_lo, core), grp: 8 (over y_hi, x).
Axes of the slice: x: 4, y: 4 (y_hi: 2, y_lo: 2; y = y_hi * 2 + y_lo), z: 4, core: 2. Of those that a mesh axis runs over, the one named last changes fastest.
Arguments:
- ratings: bfloat16 [2, 16, 8, 64, 256, 256], P(None, 'blk', 'grp'), may hold values from -6 to 6
- row_index: int32 [2, 16, 8, 64], P(None, 'blk', 'grp'), may hold values from 0 to 7
- col_index: int32 [2, 16, 8, 64], P(None, 'blk', 'grp'), may hold values from 0 to 63
- row_mask: int32 [2, 16, 8, 64, 256], P(None, 'blk', 'grp'), may hold values 0 or 1
- counts: int32 [2, 16, 8], P(None, 'blk', 'grp'), may hold values from 21 to 64, as said below
- owner_list: int32 [2, 16], P(None, 'blk'), may hold values from 0 to 7
- user_factors: float32 [262144, 128], P(('blk', 'grp'))
- item_factors: float32 [262144, 128], P('blk'), may hold values from -2 to 2
Outputs:
- user_final: float32 [262144, 128], P(('blk', 'grp'))
- item_final: float32 [262144, 128], P(('blk', 'grp'))
Inputs may be any that keep to these rules, and one draw needn't show every extreme that they name: `counts`: in every sub-epoch some device has exactly 64 live slots, and every device has at least a third of 64, rounded down.
All inputs are finite; a program needn't handle non-finite values. No bound on the sum of `row_mask` on one device may be relied on, other than what follows from the above.
Results may differ from a plain program's by a relative error of at most 0.02.
Values may be sent and summed in bfloat16 or wider, within the bound.
A program may use at most 128 MiB of HBM per device.

v0:
```python
import jax
import jax.numpy as jnp
from jax import lax
from jax.sharding import PartitionSpec as P

SUB = 2


LEARN = 0.004
GRAM = 256.0
RIDGE = 1.0


def spread(value, axis, source):
    kept = jnp.where(lax.axis_index(axis) == source, value, 0).astype(value.dtype)
    return lax.psum(kept, axis)


def passed_along(shard, axis, by):
    length = lax.axis_size(axis)
    return lax.ppermute(shard, axis, [(i, (i + by) % length) for i in range(length)])


def inner_gram(matrix):
    return lax.dot_general(
        matrix, matrix, (((0,), (0,)), ((), ())), preferred_element_type=jnp.float32
    )


def local(ratings, row_index, col_index, row_mask, counts, owner_list, user_factors, item_factors):
    members = lax.axis_size("grp")
    member_id = lax.axis_index("grp")
    tile = ratings.shape[-1]
    rank = user_factors.shape[1]
    user_rows = user_factors.shape[0]
    identity = jnp.eye(rank, dtype=jnp.float32)
    item_block = item_factors
    users_now = user_factors
    for epoch in range(SUB):
        item_bf = item_block.astype(jnp.bfloat16)
        block_rows = item_bf.shape[0]
        user_bf = users_now.astype(jnp.bfloat16)
        user_tiles = user_bf.reshape(-1, tile, rank)
        item_tiles = item_bf.reshape(-1, tile, rank)
        tile_vals = ratings[epoch, 0, 0]
        rows_in = row_index[epoch, 0, 0]
        cols_in = col_index[epoch, 0, 0]
        mask_in = row_mask[epoch, 0, 0]

        def tile_step(slot, carry):
            grad_user, grad_item = carry
            row_tile = rows_in[slot]
            col_tile = cols_in[slot]
            user_part = user_tiles[row_tile]
            item_part = item_tiles[col_tile]
            predicted = lax.dot_general(
                user_part, item_part, (((1,), (1,)), ((), ())), preferred_element_type=jnp.float32
            )
            weights = mask_in[slot].astype(jnp.float32)[:, None]
            errors = (weights * (predicted - tile_vals[slot].astype(jnp.float32))).astype(
                jnp.bfloat16
            )
            user_add = jnp.dot(errors, item_part, preferred_element_type=jnp.float32)
            item_add = lax.dot_general(
                errors, user_part, (((0,), (0,)), ((), ())), preferred_element_type=jnp.float32
            )
            grad_user = grad_user.at[row_tile].add(user_add)
            grad_item = grad_item.at[col_tile].add(item_add)
            return (grad_user, grad_item)

        start_user = jnp.zeros(user_tiles.shape, jnp.float32)
        start_item = jnp.zeros(item_tiles.shape, jnp.float32)
        grad_user, grad_item = lax.fori_loop(
            0, counts[epoch, 0, 0], tile_step, (start_user, start_item)
        )
        own_gram = inner_gram(user_bf) * (GRAM / user_rows) + RIDGE * identity
        owner_now = owner_list[epoch, 0]
        owner_gram = spread(own_gram.astype(jnp.bfloat16), "grp", owner_now).astype(own_gram.dtype)
        item_gram = inner_gram(item_bf) * (GRAM / block_rows) + RIDGE * identity
        user_pull = jnp.dot(users_now, item_gram, precision=lax.Precision.HIGHEST)
        users_now = users_now - LEARN * (grad_user.reshape(users_now.shape) + user_pull)
        item_terms = grad_item.reshape(block_rows, rank)
        item_grad = lax.psum(item_terms.astype(jnp.bfloat16), "grp").astype(jnp.float32)
        item_pull = jnp.dot(item_block, owner_gram, precision=lax.Precision.HIGHEST)
        item_block = item_block - LEARN * (item_grad + item_pull)
        item_block = passed_along(item_block.astype(jnp.bfloat16), "blk", 1).astype(
            item_block.dtype
        )
    shard_rows = item_block.shape[0] // members
    item_final = lax.dynamic_slice_in_dim(item_block, member_id * shard_rows, shard_rows, 0)
    return (users_now, item_final)


def solution(mesh):
    in_specs = (
        P(None, "blk", "grp", None, None, None),
        P(None, "blk", "grp", None),
        P(None, "blk", "grp", None),
        P(None, "blk", "grp", None, None),
        P(None, "blk", "grp"),
        P(None, "blk"),
        P(("blk", "grp"), None),
        P("blk", None),
    )
    out_specs = (P(("blk", "grp"), None), P(("blk", "grp"), None))
    return jax.shard_map(local, mesh=mesh, in_specs=in_specs, out_specs=out_specs, check_vma=False)
```

profile of v0, /device:TPU:0, one launch (start us, length us, event | category | flops | bytes accessed | tf_op | source)
XLA Modules:
  0.0 2004.4 jit_solution(13097063985972410134)
XLA Ops:
  8.5 2.5 copy.11
  11.0 11.5 slice_bitcast_fusion
  22.6 5.1 convert_element_type.99
  28.4 4.8 fusion.53
  33.2 4.2 broadcast.83.clone
  37.6 707.3 %while.28 = (s32[]{:T(128)}, f32[8,256,128]{2,1,0:T(8,128)S(1)}, f32[64,256,128]{2,1,0:T(8,128)}, s32[]{:T(128)}, s32[64]{0:T(128)S(1)}, /*index=5*/s32[64,256]{...) while((s32[]{:T(128)}, f32[8,256,128]{2,1,0:T(8,128)S(1)}, ...), condition=%wide.region_3.0_spmd, body=%wide.region_0.0_spmd.sunk | while | flops 50725164 | bytes 1318217 | solution.py:73
  68.8 2.5 fusion.110
  92.3 2.5 fusion.110
  104.1 2.5 fusion.110
  139.4 2.5 fusion.110
  162.9 2.5 fusion.110
  174.7 2.5 fusion.110
  186.5 2.5 fusion.110
  198.3 2.5 fusion.110
  210.1 2.5 fusion.110
  221.8 2.5 fusion.110
  233.6 2.5 fusion.110
  268.9 2.5 fusion.110
  280.7 2.5 fusion.110
  304.3 2.5 fusion.110
  316.1 2.5 fusion.110
  327.8 2.5 fusion.110
  339.6 2.5 fusion.110
  374.9 2.5 fusion.110
  386.7 2.5 fusion.110
  398.5 2.5 fusion.110
  422.1 2.5 fusion.110
  433.8 2.5 fusion.110
  457.4 2.5 fusion.110
  469.2 2.5 fusion.110
  481.0 2.5 fusion.110
  504.5 2.5 fusion.110
  516.3 2.5 fusion.110
  551.6 2.5 fusion.110
  563.4 2.5 fusion.110
  575.2 2.5 fusion.110
  587.0 2.5 fusion.110
  598.7 2.5 fusion.110
  622.3 2.5 fusion.110
  645.9 2.5 fusion.110
  657.7 2.5 fusion.110
  669.4 2.5 fusion.110
  681.2 2.5 fusion.110
  693.0 2.5 fusion.110
  716.5 2.5 fusion.110
  728.3 2.5 fusion.110
  740.1 2.5 fusion.110
  749.1 2.7 fusion.60
  752.7 6.1 convert_element_type.102
  758.8 6.4 copy.26
  765.5 9.0 copy.13
  774.5 110.8 %all-reduce.9.cloned.1.call-done = (bf16[128,128]{1,0:T(8,128)(2,1)}, bf16[128,128]{1,0:T(8,128)(2,1)}) async-done(((bf16[128,128]{1,0:T(8,128)(2,1)}, bf16[128,128]{1,0:T(8,128)(2,1)}), (bf16[128,128]{1,0:T(8,128)(2,1)}, bf16[128,128]{1,0:T(8,128)(2,1)})) %all-reduce.9.cloned.1.call-update) | async-done | bytes 65552 | tf_op jit(solution)/shard_map/psum | solution.py:16
  885.2 110.2 %all-reduce.5.cloned.1.call-done = bf16[16384,128]{0,1:T(8,128)(2,1)} async-done(((bf16[16384,128]{0,1:T(8,128)(2,1)}), bf16[16384,128]{0,1:T(8,128)(2,1)}) %all-reduce.5.cloned.1.call-update) | async-done | bytes 4194320 | tf_op jit(solution)/shard_map/psum | solution.py:83
  995.5 14.4 fusion.44
  1010.1 50.1 %collective-permute-done = bf16[16384,128]{0,1:T(8,128)(2,1)} collective-permute-done((bf16[16384,128]{0,1:T(8,128)(2,1)}, bf16[16384,128]{0,1:T(8,128)(2,1)}, u32[]{:S(2)}, u32[]{:S(2)}) %collective-permute-start) | collective-permute-done | bytes 4194336 | tf_op jit(solution)/shard_map/ppermute | solution.py:21
  1060.2 6.4 copy.27
  1066.6 4.3 broadcast.83
  1070.9 630.1 %while.29 = (s32[]{:T(128)}, f32[8,256,128]{2,1,0:T(8,128)S(1)}, f32[64,256,128]{2,1,0:T(8,128)}, s32[]{:T(128)}, s32[64]{0:T(128)S(1)}, /*index=5*/s32[64,256]{...) while((s32[]{:T(128)}, f32[8,256,128]{2,1,0:T(8,128)S(1)}, ...), condition=%wide.region_9.10_spmd, body=%wide.region_6.9_spmd.sunk | while | flops 50725164 | bytes 1318217 | solution.py:73
  1701.1 6.1 convert_element_type.108
  1707.1 6.4 copy.29
  1713.6 222.7 %all-reduce.7.cloned.1.call-done = bf16[16384,128]{0,1:T(8,128)(2,1)} async-done(((bf16[16384,128]{0,1:T(8,128)(2,1)}), bf16[16384,128]{0,1:T(8,128)(2,1)}) %all-reduce.7.cloned.1.call-update) | async-done | bytes 4194320 | tf_op jit(solution)/shard_map/psum | solution.py:83
  1936.2 8.8 subtract_convert_fusion
  1945.4 4.7 fusion.51
  1952.5 42.9 %collective-permute-done.1 = bf16[16384,128]{0,1:T(8,128)(2,1)} collective-permute-done((bf16[16384,128]{0,1:T(8,128)(2,1)}, bf16[16384,128]{0,1:T(8,128)(2,1)}, u32[]{:S(2)}, u32[]{:S(2)}) %collective-permute-start.1) | collective-permute-done | bytes 4194336 | tf_op jit(solution)/shard_map/ppermute | solution.py:21
  (799 shorter events, 732.3 us)
Async XLA Ops:
  7.2 878.1 %all-reduce.9.cloned.1.call-start = ((), (), s32[]{:S(2)}) async-start(), calls=%async_computation.2 | async-start | bytes 131072 | tf_op jit(solution)/shard_map/psum | solution.py:16
  22.6 5.2 copy-start.1
  22.6 5.2 copy-start.5
  27.7 5.4 copy-start.7
  27.7 5.4 copy-start.8
  33.2 4.4 copy-start.2
  33.2 4.4 copy-start.3
  33.2 713.0 %copy-start.6 = (s32[2,1]{0,1:T(1,128)S(1)}, s32[2,1]{0,1:T(1,128)}, u32[]{:S(2)}) copy-start(s32[2,1]{0,1:T(1,128)} %param.25) | copy-start | bytes 28
  33.2 715.9 %copy-start = (f32[2048,128]{1,0:T(8,128)S(1)}, f32[2048,128]{1,0:T(8,128)}, u32[]{:S(2)}) copy-start(f32[2048,128]{1,0:T(8,128)} %param.26) | copy-start | bytes 3145732
  752.7 242.8 %all-reduce.5.cloned.1.call-start = ((), (), s32[]{:S(2)}) async-start(), calls=%async_computation | async-start | bytes 8388608 | tf_op jit(solution)/shard_map/psum | solution.py:83
  765.2 1171.0 %all-reduce.7.cloned.1.call-start = ((), (), s32[]{:S(2)}) async-start(), calls=%async_computation.1 | async-start | bytes 8388608 | tf_op jit(solution)/shard_map/psum | solution.py:83
  1009.8 50.4 %collective-permute-start = (bf16[16384,128]{0,1:T(8,128)(2,1)}, bf16[16384,128]{0,1:T(8,128)(2,1)}, u32[]{:S(2)}, u32[]{:S(2)}) collective-permute-start(bf16[16384,128]{0,1:T(8,128)(2,1)} %fusion.44), channel_id=1, source_target_pairs={{0,8},{8,16},{16,24},{24,32},{32,40},{40,48},{48,56},{56,64},{64,7... | collective-permute-start | bytes 12582920 | tf_op jit(solution)/shard_map/ppermute | solution.py:21
  1707.1 229.1 %copy-start.4 = (bf16[128,128]{1,0:T(8,128)(2,1)S(1)}, bf16[128,128]{1,0:T(8,128)(2,1)}, u32[]{:S(2)}) copy-start(bf16[128,128]{1,0:T(8,128)(2,1)} %get-tuple-element.215) | copy-start | bytes 98308
  1945.0 50.4 %collective-permute-start.1 = (bf16[16384,128]{0,1:T(8,128)(2,1)}, bf16[16384,128]{0,1:T(8,128)(2,1)}, u32[]{:S(2)}, u32[]{:S(2)}) collective-permute-start(bf16[16384,128]{0,1:T(8,128)(2,1)} %subtract_convert_fusion), channel_id=1, source_target_pairs={{0,8},{8,16},{16,24},{24,32},{32,40},{40,48},{48,56},{56,64},{64,7... | collective-permute-start | bytes 12582920 | tf_op jit(solution)/shard_map/ppermute | solution.py:21
Sparse Core Ops, SparseCore 0:
  752.8 132.3 all-reduce.8
  887.9 107.5 all-reduce.4
  1713.7 222.4 all-reduce.6
where the time goes:
time: 2020 us; the launch traced here: 2000 us
  matrix products  631 us (31%)
  waiting for transfers between devices  537 us (27%)
  loops' own time  515 us (25%)
  local copies, waits for them, and re-layouts  195 us (10%)
  other arithmetic  111 us (5%)
    another operation x2, loops' own time, local(): lax.fori_loop(0, counts[epoch, 0, 0], tile_step, (start_user, start_item))  515 us
    psum x2, waiting for transfers between devices, local(): lax.psum(item_terms.astype(jnp.bfloat16), 'grp').astype(jnp.float32)  333 us
    dot_general x114, matrix products, tile_step(): lax.dot_general(errors, user_part, (((0,), (0,)), ((), ())), preferred_el...  275 us
    dot_general x114, matrix products, tile_step(): user_add = jnp.dot(errors, item_part, preferred_element_type=jnp.float32)  187 us
    dot_general x114, matrix products, tile_step(): lax.dot_general(user_part, item_part, (((1,), (1,)), ((), ())), preferred...  130 us
    psum x1, waiting for transfers between devices, spread(): return lax.psum(kept, axis)  111 us
    ppermute x2, waiting for transfers between devices, passed_along(): lax.ppermute(shard, axis, [(i, (i + by) % length) for i in range(length)])  92.9 us
    another operation x114, other arithmetic  89.7 us
  transfers between devices with their start and end apart: 5, of which 5 were waited for; matrix products, arithmetic and copies ran while one was open for 1% of the time, Pallas kernels for 0%

commit v1 on v0

v1 whole, which is shorter than its diff:
```python
import functools

import jax
import jax.numpy as jnp
from jax import lax
from jax.experimental import pallas as pl
from jax.experimental.pallas import tpu as pltpu
from jax.sharding import PartitionSpec as P

LEARN = 0.004
GRAM = 256.0
RIDGE = 1.0

TILE = 256
RANK = 128
SLOTS = 64
USER_TILES = 8
ITEM_TILES = 64
OWNERS = 8
GROUP = 4

SUM_ROWS = 1024
SUM_P = 576
SUM_Q = SUM_ROWS - SUM_P
OUT_ROWS = 2048
OUT_P = 1152
OUT_Q = OUT_ROWS - OUT_P
STEP = 32

F32, BF16, I32 = jnp.float32, jnp.bfloat16, jnp.int32
MESH = pl.DeviceIdType.MESH


def dot(a, b, ca=1, cb=0, precision=None):
    return lax.dot_general(
        a, b, (((ca,), (cb,)), ((), ())), precision=precision, preferred_element_type=F32
    )


def ridge():
    row = lax.broadcasted_iota(I32, (RANK, RANK), 0)
    col = lax.broadcasted_iota(I32, (RANK, RANK), 1)
    return jnp.where(row == col, RIDGE, 0.0).astype(F32)


def grads_kernel(
    epoch, rows, cols, counts, ratings, mask, users, items, part_out, users_out, gram_out,
    order, tally, rbuf, vbuf, err, part, acc, ub, ubt, ug, gram, rsem, vsem, osem,
):
    live_count = counts[epoch]
    items_in = pltpu.make_async_copy(items, vbuf, vsem)
    items_in.start()

    def key(t):
        return jnp.where(t < live_count, cols[epoch, t], ITEM_TILES)

    @pl.loop(0, ITEM_TILES + 1)
    def _(j):
        tally[j] = 0

    @pl.loop(0, SLOTS)
    def _(t):
        tally[key(t)] = tally[key(t)] + 1

    def running(j, total):
        here = tally[j]
        tally[j] = total
        return total + here

    lax.fori_loop(0, ITEM_TILES + 1, running, 0)

    @pl.loop(0, SLOTS)
    def _(t):
        place = tally[key(t)]
        tally[key(t)] = place + 1
        order[place] = t
        pltpu.make_async_copy(ratings.at[epoch, t], rbuf.at[place], rsem.at[place]).start()

    for i in range(USER_TILES):
        u = users[pl.ds(i * TILE, TILE), :]
        ub[i] = u.astype(BF16)
        ubt[i] = u.T.astype(BF16)
    own = jnp.zeros((RANK, RANK), F32)
    for i in range(USER_TILES):
        own = own + dot(ubt[i], ub[i])
    gram_out[...] = (own * (GRAM / OUT_ROWS) + ridge()).astype(BF16)

    @pl.loop(0, ITEM_TILES)
    def _(j):
        part[j] = jnp.zeros((RANK, TILE), BF16)

    ug[...] = jnp.zeros_like(ug)
    acc[...] = jnp.zeros_like(acc)
    gram[...] = jnp.zeros_like(gram)
    items_in.wait()

    def errors(p):
        t = order[p]
        pltpu.make_async_copy(ratings.at[epoch, 0], rbuf.at[p], rsem.at[p]).wait()
        predicted = dot(ub[rows[epoch, t]], vbuf[cols[epoch, t]].astype(BF16), 1, 1)
        err[p] = (predicted - rbuf[p].astype(F32)).astype(BF16)

    def weights(t):
        live = jnp.where(t < live_count, 1.0, 0.0)
        return mask[epoch, pl.ds(t, 1), :].astype(F32) * live

    def item_side(p, before):
        t = order[p]
        j = key(t)
        add = dot(ubt[rows[epoch, t]] * weights(t).astype(BF16), err[p])
        total = acc[...] * jnp.where(j == before, 1.0, 0.0) + add
        acc[...] = total
        part[j] = total.astype(BF16)
        return j

    def user_side(p):
        t = order[p]
        i = rows[epoch, t]
        add = dot(vbuf[cols[epoch, t]].astype(BF16), err[p], 0, 1)
        ug[i] = ug[i] + add * weights(t)

    def gram_side(j):
        v = vbuf[j].astype(BF16)
        gram[...] += dot(v, v, 0, 0)

    for q in range(GROUP):
        errors(q)

    def step(g, before):
        for q in range(GROUP):
            before = item_side(g * GROUP + q, before)
        for q in range(GROUP):
            user_side(g * GROUP + q)
        for q in range(GROUP):
            errors(g * GROUP + GROUP + q)
        for q in range(GROUP):
            gram_side(g * GROUP + q)
        return before

    before = lax.fori_loop(0, SLOTS // GROUP - 1, step, -1)
    for q in range(GROUP):
        before = item_side(SLOTS - GROUP + q, before)
    out = pltpu.make_async_copy(part.at[pl.ds(0, ITEM_TILES)], part_out, osem)
    out.start()
    for q in range(GROUP):
        user_side(SLOTS - GROUP + q)
        gram_side(SLOTS - GROUP + q)
    pull = gram[...] * (GRAM / (ITEM_TILES * TILE)) + ridge()

    @pl.loop(0, USER_TILES)
    def _(i):
        u = users[pl.ds(i * TILE, TILE), :]
        pulled = dot(u, pull, precision=lax.Precision.HIGHEST)
        users_out[pl.ds(i * TILE, TILE), :] = u - LEARN * (ug[i].T + pulled)

    out.wait()


def grads(epoch, rows, cols, counts, ratings, mask, users, items):
    smem = pl.BlockSpec(memory_space=pltpu.SMEM)
    vmem = pl.BlockSpec(memory_space=pltpu.VMEM)
    anywhere = pl.BlockSpec(memory_space=pl.ANY)
    dma = pltpu.SemaphoreType.DMA
    return pl.pallas_call(
        functools.partial(grads_kernel, epoch),
        out_shape=[
            jax.ShapeDtypeStruct((ITEM_TILES, RANK, TILE), BF16),
            jax.ShapeDtypeStruct(users.shape, F32),
            jax.ShapeDtypeStruct((RANK, RANK), BF16),
        ],
        in_specs=[smem, smem, smem, anywhere, vmem, vmem, anywhere],
        out_specs=[anywhere, vmem, vmem],
        scratch_shapes=[
            pltpu.SMEM((SLOTS,), I32),
            pltpu.SMEM((ITEM_TILES + 1,), I32),
            pltpu.VMEM((SLOTS, TILE, TILE), BF16),
            pltpu.VMEM((ITEM_TILES, TILE, RANK), items.dtype),
            pltpu.VMEM((SLOTS, TILE, TILE), BF16),
            pltpu.VMEM((ITEM_TILES + 1, RANK, TILE), BF16),
            pltpu.VMEM((RANK, TILE), F32),
            pltpu.VMEM((USER_TILES, TILE, RANK), BF16),
            pltpu.VMEM((USER_TILES, RANK, TILE), BF16),
            pltpu.VMEM((USER_TILES, RANK, TILE), F32),
            pltpu.VMEM((RANK, RANK), F32),
            dma((SLOTS,)),
            dma,
            dma,
        ],
        compiler_params=pltpu.CompilerParams(vmem_limit_bytes=48 * 2**20),
        name="grads%d" % epoch,
    )(rows, cols, counts, ratings, mask, users, items)


def places():
    b, g = lax.axis_index("blk"), lax.axis_index("grp")
    blocks = lax.axis_size("blk")
    x, yh = g % 4, g // 4
    xp, xm, xo, yo = (x + 1) % 4, (x + 3) % 4, (x + 2) % 4, 1 - yh
    x1 = x + 1 - 2 * (x % 2)
    return dict(
        b=b, g=g, x=x, yh=yh, xp=xp, xm=xm, xo=xo, yo=yo,
        to_xp=(b, yh * 4 + xp), to_xm=(b, yh * 4 + xm), to_xo=(b, yh * 4 + xo),
        to_x1=(b, yh * 4 + x1), to_y=(b, yo * 4 + x),
        to_next=((b + 1) % blocks, g), to_last=((b + blocks - 1) % blocks, g),
    )


def add_rows(count, fn):
    @pl.loop(0, count // STEP)
    def _(k):
        fn(pl.ds(pl.multiple_of(k * STEP, STEP), STEP))


class Copies:
    def __init__(self, send, recv):
        self.send, self.recv, self.made = send, recv, []

    def start(self, src, dst, to):
        k = len(self.made)
        copy = pltpu.make_async_remote_copy(
            src_ref=src, dst_ref=dst, send_sem=self.send.at[k], recv_sem=self.recv.at[k],
            device_id=to, device_id_type=MESH,
        )
        copy.start()
        self.made.append(copy)
        return copy

    def finish(self):
        for copy in self.made:
            copy.wait_send()


COPIES = 45


def exchange_kernel(
    epoch, last, owner, part, gram_in, items, out,
    r1p, r1m, r2p, r2m, rq, q1p, q1m, q2p, q2m, ry, gsend, grecv, base, total, newv, landing, send, recv,
):
    w = places()
    x, yh, xp, xm, xo, yo = (w[k] for k in ("x", "yh", "xp", "xm", "xo", "yo"))
    barrier = pltpu.get_barrier_semaphore()
    peers = ("to_xp", "to_xm", "to_xo", "to_y", "to_next", "to_last")
    for peer in peers:
        pl.semaphore_signal(barrier, inc=1, device_id=w[peer], device_id_type=MESH)
    gsend[0] = jnp.where(owner[epoch] == w["g"], gram_in[...], jnp.zeros_like(gram_in))
    pl.semaphore_wait(barrier, len(peers))
    copies = Copies(send, recv)
    half_p, half_q = SUM_P // 2, SUM_Q // 2
    pa, pb = pl.ds(0, half_p), pl.ds(half_p, half_p)
    p_rows, q_rows = pl.ds(0, SUM_P), pl.ds(SUM_P, SUM_Q)

    def own(a, b):
        return a * 4 + b

    c_g0 = copies.start(gsend.at[0], grecv.at[0], w["to_y"])
    c_1p = [copies.start(part.at[own(a, xo), pa], r1p.at[a], w["to_xp"]) for a in range(2)]
    c_1m = [copies.start(part.at[own(a, xo), pb], r1m.at[a], w["to_xm"]) for a in range(2)]
    c_q = [copies.start(part.at[own(yo, d), q_rows], rq.at[d], w["to_y"]) for d in (xo, xp, xm, x)]
    c_2pb = [copies.start(part.at[own(a, xp), pb], r2p.at[a, pb], w["to_xp"]) for a in range(2)]
    c_2ma = [copies.start(part.at[own(a, xm), pa], r2m.at[a, pa], w["to_xm"]) for a in range(2)]

    c_2pa, c_2mb = [], []
    for a in range(2):
        c_1p[a].wait_recv()

        def fn(s, a=a):
            r1p[a, s, :] = (r1p[a, s, :].astype(F32) + part[own(a, xp), s, :].astype(F32)).astype(BF16)

        add_rows(half_p, fn)
        c_2pa.append(copies.start(r1p.at[a], r2p.at[a, pa], w["to_xp"]))
        c_1m[a].wait_recv()

        def fn(s, a=a):
            t = pl.ds(pl.multiple_of(s.start + half_p, STEP), STEP)
            r1m[a, s, :] = (r1m[a, s, :].astype(F32) + part[own(a, xm), t, :].astype(F32)).astype(BF16)

        add_rows(half_p, fn)
        c_2mb.append(copies.start(r1m.at[a], r2m.at[a, pb], w["to_xm"]))

    c_g0.wait_recv()
    gsend[1] = gsend[0] + grecv[0]
    c_g1 = copies.start(gsend.at[1], grecv.at[1], w["to_x1"])

    def sum_q(d):
        def fn(s):
            t = pl.ds(pl.multiple_of(s.start + SUM_P, STEP), STEP)
            rq[d, s, :] = (rq[d, s, :].astype(F32) + part[own(yh, d), t, :].astype(F32)).astype(BF16)

        add_rows(SUM_Q, fn)

    qa, qb = pl.ds(0, half_q), pl.ds(half_q, half_q)
    c_q[0].wait_recv()
    sum_q(xo)
    c_q1p = copies.start(rq.at[xo, qa], q1p, w["to_xp"])
    c_q1m = copies.start(rq.at[xo, qb], q1m, w["to_xm"])
    c_g1.wait_recv()
    gsend[2] = gsend[1] + grecv[1]
    c_g2 = copies.start(gsend.at[2], grecv.at[2], w["to_xo"])
    c_q[1].wait_recv()
    sum_q(xp)
    c_q2pb = copies.start(rq.at[xp, qb], q2p.at[qb], w["to_xp"])
    c_q[2].wait_recv()
    sum_q(xm)
    c_q2ma = copies.start(rq.at[xm, qa], q2m.at[qa], w["to_xm"])

    def sum_p(a):
        def fn(s):
            both = r2p[a, s, :].astype(F32) + r2m[a, s, :].astype(F32)
            return both + part[own(a, x), s, :].astype(F32)

        return fn

    for a in range(2):
        c_2pb[a].wait_recv()
        c_2ma[a].wait_recv()
        c_2pa[a].wait_recv()
        c_2mb[a].wait_recv()
    other, mine = sum_p(yo), sum_p(yh)

    def fn(s):
        r2p[yo, s, :] = other(s).astype(BF16)

    add_rows(SUM_P, fn)
    c_y = copies.start(r2p.at[yo], ry, w["to_y"])

    c_q1p.wait_recv()

    def fn(s):
        q1p[s, :] = (q1p[s, :].astype(F32) + rq[xp, s, :].astype(F32)).astype(BF16)

    add_rows(half_q, fn)
    c_q2pa = copies.start(q1p, q2p.at[qa], w["to_xp"])
    c_q1m.wait_recv()

    def fn(s):
        t = pl.ds(pl.multiple_of(s.start + half_q, STEP), STEP)
        q1m[s, :] = (q1m[s, :].astype(F32) + rq[xm, t, :].astype(F32)).astype(BF16)

    add_rows(half_q, fn)
    c_q2mb = copies.start(q1m, q2m.at[qb], w["to_xm"])

    c_q[3].wait_recv()
    sum_q(x)
    c_g2.wait_recv()
    pull = (gsend[2] + grecv[2]).astype(F32)

    @pl.loop(0, OUT_ROWS // TILE)
    def _(k):
        s = pl.ds(pl.multiple_of(k * TILE, TILE), TILE)
        v = items[s, :].astype(F32)
        base[s, :] = v - LEARN * dot(v, pull, precision=lax.Precision.HIGHEST)

    def fn(s):
        total[s, :] = mine(s)

    add_rows(SUM_P, fn)
    c_y.wait_recv()

    def fn(s):
        total[s, :] = total[s, :] + ry[s, :].astype(F32)

    add_rows(SUM_P, fn)
    for c in (c_q2pb, c_q2ma, c_q2pa, c_q2mb):
        c.wait_recv()

    def fn(s):
        t = pl.ds(pl.multiple_of(s.start + SUM_P, STEP), STEP)
        total[t, :] = rq[x, s, :].astype(F32) + (q2p[s, :].astype(F32) + q2m[s, :].astype(F32))

    add_rows(SUM_Q, fn)

    def update(k):
        s = pl.ds(k * TILE, TILE)
        newv[s, :] = (base[s, :] - LEARN * total[pl.ds(k * RANK, RANK), :].T).astype(BF16)

    for k in range(OUT_ROWS // TILE):
        update(k)
    if last:
        c_v = copies.start(newv, landing, w["to_next"])
        c_v.wait_recv()

        @pl.loop(0, OUT_ROWS // TILE)
        def _(k):
            s = pl.ds(pl.multiple_of(k * TILE, TILE), TILE)
            out[s, :] = landing[s, :].astype(F32)

        copies.finish()
        return

    half_p, half_q = OUT_P // 2, OUT_Q // 2
    p, pa, pb = pl.ds(0, OUT_P), pl.ds(0, half_p), pl.ds(half_p, half_p)
    q, qa, qb = pl.ds(OUT_P, OUT_Q), pl.ds(OUT_P, half_q), pl.ds(OUT_P + half_q, half_q)
    me = w["g"]
    c_vp = copies.start(newv.at[p], out.at[me, p], w["to_next"])
    c_vq = copies.start(newv.at[q], out.at[me, q], w["to_next"])

    def along(o, rows, to):
        return copies.start(out.at[o, rows], out.at[o, rows], w[to])

    c_vp.wait_recv()
    c_py = along(me, p, "to_y")
    c_pp = [along(me, p, "to_xp")]
    c_pm = [along(me, p, "to_xm")]
    c_vq.wait_recv()
    c_qp = along(me, q, "to_xp")
    c_qm = along(me, q, "to_xm")
    c_qy = [along(me, q, "to_y")]
    c_py.wait_recv()
    c_pp.append(along(own(yo, x), p, "to_xp"))
    c_pm.append(along(own(yo, x), p, "to_xm"))
    c_pp[0].wait_recv()
    c_fp = [along(own(yh, xm), pa, "to_xp")]
    c_pm[0].wait_recv()
    c_fm = [along(own(yh, xp), pb, "to_xm")]
    c_qp.wait_recv()
    c_qy.append(along(own(yh, xm), q, "to_y"))
    c_qfp = along(own(yh, xm), qa, "to_xp")
    c_qm.wait_recv()
    c_qy.append(along(own(yh, xp), q, "to_y"))
    c_qfm = along(own(yh, xp), qb, "to_xm")
    c_pp[1].wait_recv()
    c_fp.append(along(own(yo, xm), pa, "to_xp"))
    c_pm[1].wait_recv()
    c_fm.append(along(own(yo, xp), pb, "to_xm"))
    c_qfp.wait_recv()
    c_qfm.wait_recv()
    c_qy.append(along(own(yh, xo), q, "to_y"))
    for c in c_fp + c_fm + c_qy:
        c.wait_recv()
    copies.finish()


def exchange(epoch, last, owner, part, gram, items):
    smem = pl.BlockSpec(memory_space=pltpu.SMEM)
    vmem = pl.BlockSpec(memory_space=pltpu.VMEM)
    dma = pltpu.SemaphoreType.DMA
    if last:
        out = jax.ShapeDtypeStruct((OUT_ROWS, RANK), F32)
    else:
        out = jax.ShapeDtypeStruct((OWNERS, OUT_ROWS, RANK), BF16)

    def wide(*rows):
        return pltpu.VMEM((*rows, TILE), BF16)

    return pl.pallas_call(
        functools.partial(exchange_kernel, epoch, last),
        out_shape=out,
        in_specs=[smem, vmem, vmem, vmem],
        out_specs=vmem,
        scratch_shapes=[
            wide(2, SUM_P // 2), wide(2, SUM_P // 2), wide(2, SUM_P), wide(2, SUM_P),
            wide(4, SUM_Q), wide(SUM_Q // 2), wide(SUM_Q // 2), wide(SUM_Q), wide(SUM_Q), wide(SUM_P),
            pltpu.VMEM((3, RANK, RANK), BF16),
            pltpu.VMEM((3, RANK, RANK), BF16),
            pltpu.VMEM((OUT_ROWS, RANK), F32),
            pltpu.VMEM((SUM_ROWS, TILE), F32),
            pltpu.VMEM((OUT_ROWS, RANK), BF16),
            pltpu.VMEM((OUT_ROWS, RANK), BF16),
            dma((COPIES,)),
            dma((COPIES,)),
        ],
        compiler_params=pltpu.CompilerParams(
            collective_id=epoch, has_side_effects=True, vmem_limit_bytes=48 * 2**20
        ),
        name="exchange%d" % epoch,
    )(owner, part, gram, items)


def local(ratings, row_index, col_index, row_mask, counts, owner_list, user_factors, item_factors):
    epochs = ratings.shape[0]
    ratings = ratings.reshape(epochs, SLOTS, TILE, TILE)
    rows = row_index.reshape(epochs, SLOTS)
    cols = col_index.reshape(epochs, SLOTS)
    mask = row_mask.reshape(epochs, SLOTS, TILE)
    counts = counts.reshape(epochs)
    owner = owner_list.reshape(epochs)
    users = user_factors
    member = lax.axis_index("grp")
    items = item_factors.reshape(ITEM_TILES, TILE, RANK)
    for epoch in range(epochs):
        part, users, gram = grads(epoch, rows, cols, counts, ratings, mask, users, items)
        part = part.reshape(OWNERS, SUM_ROWS, TILE)
        mine = lax.dynamic_slice_in_dim(items.reshape(OWNERS, OUT_ROWS, RANK), member, 1, 0)[0]
        last = epoch == epochs - 1
        moved = exchange(epoch, last, owner, part, gram, mine)
        items = moved if last else moved.reshape(ITEM_TILES, TILE, RANK)
    return users, items


def solution(mesh):
    in_specs = (
        P(None, "blk", "grp", None, None, None),
        P(None, "blk", "grp", None),
        P(None, "blk", "grp", None),
        P(None, "blk", "grp", None, None),
        P(None, "blk", "grp"),
        P(None, "blk"),
        P(("blk", "grp"), None),
        P("blk", None),
    )
    out_specs = (P(("blk", "grp"), None), P(("blk", "grp"), None))
    return jax.shard_map(local, mesh=mesh, in_specs=in_specs, out_specs=out_specs, check_vma=False)
```

time: 2020 us -> 190 us (0.09)
  matrix products: 631 us -> 0 us
  waiting for transfers between devices: 537 us -> 0 us
  loops' own time: 515 us -> 0 us
  local copies, waits for them, and re-layouts: 195 us -> 9.46 us
  Pallas kernels: 0 us -> 178 us
  other arithmetic: 111 us -> 0 us
    dot_general x350 -> x0, matrix products: 631 us -> none  [the longest x114 275 us: tile_step(): lax.dot_general(errors, user_part, (((0,), (0,)), ((), ())), preferred_el...]
    another operation x2 -> x0, loops' own time: 515 us -> none  [local(): lax.fori_loop(0, counts[epoch, 0, 0], tile_step, (start_user, start_item))]
    psum x3 -> x0, waiting for transfers between devices: 444 us -> none  [the longest x2 333 us: local(): lax.psum(item_terms.astype(jnp.bfloat16), 'grp').astype(jnp.float32)]
    pallas_call x0 -> x4, Pallas kernels: none -> 178 us  [the longest x2 119 us: exchange(): pl.pallas_call(functools.partial(exchange_kernel, epoch, last), out_shape...]
    dynamic_slice x228 -> x0, local copies, waits for them, and re-layouts: 139 us -> none  [the longest x114 71.1 us: tile_step(): row_tile = rows_in[slot]]
    ppermute x2 -> x0, waiting for transfers between devices: 92.9 us -> none  [passed_along(): lax.ppermute(shard, axis, [(i, (i + by) % length) for i in range(length)])]
    another operation x114 -> x0, other arithmetic: 89.7 us -> none
    convert_element_type x119 -> x0, other arithmetic: 21.2 us -> none  [the longest x2 12.2 us: local(): item_terms.astype(jnp.bfloat16)]
  transfers between devices with their start and end apart: 5 -> 0, of which waited for: 5 -> 0; matrix products, arithmetic and copies ran while one was open for 1% -> 0% of each run, Pallas kernels for 0% -> 0%
where the time goes in v1:
time: 190 us; the launch traced here: 189 us
  Pallas kernels  178 us (94%)
  local copies, waits for them, and re-layouts  9.46 us (5%)
    pallas_call x2, Pallas kernels, exchange(): pl.pallas_call(functools.partial(exchange_kernel, epoch, last), out_shape...  119 us
    pallas_call x2, Pallas kernels, grads(): pl.pallas_call(functools.partial(grads_kernel, epoch), out_shape=[jax.Sha...  59.6 us
    unnamed x23, local copies, waits for them, and re-layouts  7.08 us

profile of v1, /device:TPU:0, one launch (start us, length us, event | category | flops | bytes accessed | tf_op | source)
XLA Modules:
  0.0 188.5 jit_solution(4063790613565493027)
XLA Ops:
  0.6 0.0 copy-start.1
  0.6 1.2 copy-done.1
  1.9 0.0 copy-start.2
  1.9 0.9 copy-done.2
  2.8 0.0 copy-start.4
  2.8 0.7 copy-done.4
  3.4 0.0 copy-start.6
  3.4 0.7 copy-done.6
  4.1 0.0 copy-start.8
  4.1 0.7 copy-done.8
  4.8 0.0 copy-start.10
  4.8 29.2 %grads0.1 = (bf16[64,128,256]{2,1,0:T(8,128)(2,1)}, f32[2048,128]{1,0:T(8,128)S(1)}, bf16[128,128]{1,0:T(8,128)(2,1)S(1)}) custom-call(s32[2,64]{1,0:T(2,128)S(1)} %bitcast.19, s32[2,64]{1,0:T(2,128)S(1)} %bitcast.21, s32[2]{0:T(128)S(1)} %bitcast.23, bf16[2,64,256,256]{3,2,1,0:T(8,128)(2,1)} %bitcast.27, s32[2,64,256]{2,1,0:T(8,128)S(1)} %bitcast.17, ...), custom_call_target="tpu_custom_call" | custom-call | tf_op jit(solution)/shard_map/grads0/pallas_call | solution.py:164
  34.0 1.3 dynamic-slice_bitcast_fusion.items
  35.3 0.0 copy-done.10
  35.3 0.0 copy-start.3
  35.3 0.0 copy-start.5
  35.3 0.0 copy-start.7
  35.3 0.0 copy-start.9
  35.3 75.5 %exchange0.1 = bf16[8,2048,128]{2,1,0:T(8,128)(2,1)S(1)} custom-call(s32[2]{0:T(128)S(1)} %bitcast.25, bf16[8,1024,256]{2,1,0:T(8,128)(2,1)} %bitcast.31, bf16[128,128]{1,0:T(8,128)(2,1)S(1)} %get-tuple-element.10.gram_in, f32[2048,128]{1,0:T(8,128)S(1)} %dynamic-slice_bitcast_fusion.items), custom_call_target="tpu_custom_call" | custom-call | tf_op jit(solution)/shard_map/exchange0/pallas_call | solution.py:446
  110.8 0.0 copy-start
  110.8 1.9 %copy-done = bf16[8,2048,128]{2,1,0:T(8,128)(2,1)} copy-done((bf16[8,2048,128]{2,1,0:T(8,128)(2,1)}, bf16[8,2048,128]{2,1,0:T(8,128)(2,1)S(1)}, u32[]{:S(2)}) %copy-start) | copy-done | bytes 4194328
  112.8 0.0 copy-done.3
  112.8 0.0 copy-done.5
  112.8 0.0 copy-done.7
  112.8 0.0 copy-done.9
  112.8 30.4 %grads1.1 = (bf16[64,128,256]{2,1,0:T(8,128)(2,1)S(1)}, f32[2048,128]{1,0:T(8,128)}, bf16[128,128]{1,0:T(8,128)(2,1)S(1)}) custom-call(s32[2,64]{1,0:T(2,128)S(1)} %bitcast.20, s32[2,64]{1,0:T(2,128)S(1)} %bitcast.22, s32[2]{0:T(128)S(1)} %bitcast.24, bf16[2,64,256,256]{3,2,1,0:T(8,128)(2,1)} %bitcast.28, s32[2,64,256]{2,1,0:T(8,128)S(1)} %bitcast.18, ...), custom_call_target="tpu_custom_call" | custom-call | tf_op jit(solution)/shard_map/grads1/pallas_call | solution.py:164
  143.2 1.1 dynamic-slice_bitcast_fusion.1.items
  144.3 43.2 %exchange1.1 = f32[2048,128]{1,0:T(8,128)S(1)} custom-call(s32[2]{0:T(128)S(1)} %bitcast.26, bf16[8,1024,256]{2,1,0:T(8,128)(2,1)S(1)} %bitcast.16, bf16[128,128]{1,0:T(8,128)(2,1)S(1)} %get-tuple-element.13.gram_in, bf16[2048,128]{1,0:T(8,128)(2,1)S(1)} %dynamic-slice_bitcast_fusion.1.items), custom_call_target="tpu_custom_call" | custom-call | tf_op jit(solution)/shard_map/exchange1/pallas_call | solution.py:446
  187.5 1.0 copy.11
Async XLA Ops:
  0.6 1.2 copy-start.1
  1.9 0.9 copy-start.2
  2.8 0.7 copy-start.4
  3.4 0.7 copy-start.6
  4.1 0.7 copy-start.8
  4.8 30.5 %copy-start.10 = (s32[2,1]{0,1:T(1,128)S(1)}, s32[2,1]{0,1:T(1,128)}, u32[]{:S(2)}) copy-start(s32[2,1]{0,1:T(1,128)} %param.13) | copy-start | bytes 28
  35.3 77.5 %copy-start.3 = (s32[2,1,1,64,256]{4,3,2,1,0:T(8,128)S(1)}, s32[2,1,1,64,256]{4,3,2,1,0:T(8,128)}, u32[]{:S(2)}) copy-start(s32[2,1,1,64,256]{4,3,2,1,0:T(8,128)} %param.11) | copy-start | bytes 393220
  35.3 77.5 %copy-start.5 = (s32[2,1,1,64]{3,2,1,0:T(1,128)S(1)}, s32[2,1,1,64]{3,2,1,0:T(1,128)}, u32[]{:S(2)}) copy-start(s32[2,1,1,64]{3,2,1,0:T(1,128)} %param.9) | copy-start | bytes 1540
  35.3 77.5 %copy-start.7 = (s32[2,1,1,64]{3,2,1,0:T(1,128)S(1)}, s32[2,1,1,64]{3,2,1,0:T(1,128)}, u32[]{:S(2)}) copy-start(s32[2,1,1,64]{3,2,1,0:T(1,128)} %param.10) | copy-start | bytes 1540
  35.3 77.5 %copy-start.9 = (s32[2,1,1]{0,2,1:T(1,128)S(1)}, s32[2,1,1]{0,2,1:T(1,128)}, u32[]{:S(2)}) copy-start(s32[2,1,1]{0,2,1:T(1,128)} %param.12) | copy-start | bytes 28
  110.8 2.0 %copy-start = (bf16[8,2048,128]{2,1,0:T(8,128)(2,1)}, bf16[8,2048,128]{2,1,0:T(8,128)(2,1)S(1)}, u32[]{:S(2)}) copy-start(bf16[8,2048,128]{2,1,0:T(8,128)(2,1)S(1)} %exchange0.1) | copy-start | bytes 12582916

commit v2 on v0

v2 whole, which is shorter than its diff:
```python
import functools

import jax
import jax.numpy as jnp
from jax import lax
from jax.experimental import pallas as pl
from jax.experimental.pallas import tpu as pltpu
from jax.sharding import PartitionSpec as P

LEARN = 0.004
GRAM = 256.0
RIDGE = 1.0

TILE = 256
RANK = 128
SLOTS = 64
USER_TILES = 8
ITEM_TILES = 64
OWNERS = 8
GROUP = 8
USER_ROWS = USER_TILES * TILE

WAVES = 2
HALF = RANK // WAVES
WAVE_ROWS = 8 * HALF
P_ROWS = 288
Q_ROWS = WAVE_ROWS - P_ROWS
PH, QH = P_ROWS // 2, Q_ROWS // 2
UNIT = 16
TILE_UNITS = HALF // UNIT
WAVE_UNITS = WAVE_ROWS // UNIT


def units(owner, start, rows):
    return pl.ds(owner * WAVE_UNITS + start // UNIT, rows // UNIT)


PREV_COL, PREV_ROW, COL, ROW, LAST_COL, LAST_ROW, COUNT, OWNER, TABLE = 0, 64, 128, 192, 256, 320, 328, 329, 384

F32, BF16, I32 = jnp.float32, jnp.bfloat16, jnp.int32
MESH = pl.DeviceIdType.MESH
HIGHEST = lax.Precision.HIGHEST


def dot(a, b, ca=1, cb=0, precision=None):
    return lax.dot_general(
        a, b, (((ca,), (cb,)), ((), ())), precision=precision, preferred_element_type=F32
    )


def ridge():
    row = lax.broadcasted_iota(I32, (RANK, RANK), 0)
    col = lax.broadcasted_iota(I32, (RANK, RANK), 1)
    return jnp.where(row == col, RIDGE, 0.0).astype(F32)


def table_kernel(rows, cols, counts, owner, out):
    for e in range(rows.shape[0]):
        n = counts[e]

        @pl.loop(0, SLOTS, unroll=8)
        def _(t):
            out[e, PREV_COL + t] = SLOTS
            out[e, PREV_ROW + t] = SLOTS
            out[e, LAST_COL + t] = SLOTS
            out[e, COL + t] = cols[e, t]
            out[e, ROW + t] = rows[e, t]

        for i in range(USER_TILES):
            out[e, LAST_ROW + i] = SLOTS
        out[e, COUNT] = n
        out[e, OWNER] = owner[e]

        @pl.loop(0, n)
        def _(t):
            c, r = cols[e, t], rows[e, t]
            out[e, PREV_COL + t] = out[e, LAST_COL + c]
            out[e, LAST_COL + c] = t
            out[e, PREV_ROW + t] = out[e, LAST_ROW + r]
            out[e, LAST_ROW + r] = t


def table(rows, cols, counts, owner):
    smem = pl.BlockSpec(memory_space=pltpu.SMEM)
    return pl.pallas_call(
        table_kernel,
        out_shape=jax.ShapeDtypeStruct((rows.shape[0], TABLE), I32),
        in_specs=[smem] * 4,
        out_specs=smem,
        name="table",
    )(rows, cols, counts, owner)


def places():
    b, g = lax.axis_index("blk"), lax.axis_index("grp")
    blocks = lax.axis_size("blk")
    x, yh = g % 4, g // 4
    xp, xm, xo, yo = (x + 1) % 4, (x + 3) % 4, (x + 2) % 4, 1 - yh
    x1 = x + 1 - 2 * (x % 2)
    return dict(
        b=b, g=g, x=x, yh=yh, xp=xp, xm=xm, xo=xo, yo=yo,
        to_xp=(b, yh * 4 + xp), to_xm=(b, yh * 4 + xm), to_xo=(b, yh * 4 + xo),
        to_x1=(b, yh * 4 + x1), to_y=(b, yo * 4 + x),
        to_next=((b + 1) % blocks, g), to_last=((b + blocks - 1) % blocks, g),
    )


PEERS = ("to_xp", "to_xm", "to_xo", "to_y", "to_next", "to_last")


def in_steps(count, step, fn):
    if count == step:
        fn(0)
        return

    @pl.loop(0, count // step)
    def _(k):
        fn(pl.multiple_of(k * step, step))


class Copies:
    def __init__(self, send, recv):
        self.send, self.recv, self.used, self.open = send, recv, 0, []

    def start(self, src, dst, to):
        k = self.used
        assert k < COPIES
        self.used += 1
        copy = pltpu.make_async_remote_copy(
            src_ref=src, dst_ref=dst, send_sem=self.send.at[k], recv_sem=self.recv.at[k],
            device_id=to, device_id_type=MESH,
        )
        copy.start()
        self.open.append(copy)
        return copy

    def finish(self):
        for copy in self.open:
            copy.wait_send()
        self.open = []


COPIES = 160


class Sum:
    def __init__(self, copies, w, wave, part, bufs, base, total, newv):
        self.c, self.w, self.wave = copies, w, wave
        self.part = part.at[wave]
        self.bufs = {k: v.at[wave] for k, v in bufs.items()}
        self.base, self.total, self.newv = base, total.at[wave], newv.at[wave]

    def start(self):
        w, c, part, b = self.w, self.c, self.part, self.bufs
        xp, xm, xo, yo = w["xp"], w["xm"], w["xo"], w["yo"]
        pa, pb, q = pl.ds(0, PH), pl.ds(PH, PH), pl.ds(P_ROWS, Q_ROWS)
        self.one_p = [c.start(part.at[a * 4 + xo, pa], b["r1p"].at[a], w["to_xp"]) for a in range(2)]
        self.one_m = [c.start(part.at[a * 4 + xo, pb], b["r1m"].at[a], w["to_xm"]) for a in range(2)]
        self.q = [
            c.start(part.at[yo * 4 + d, q], b["rq"].at[d], w["to_y"]) for d in (xo, xp, xm, w["x"])
        ]
        self.two = [c.start(part.at[a * 4 + xp, pb], b["r2p"].at[a, pb], w["to_xp"]) for a in range(2)]
        self.two += [c.start(part.at[a * 4 + xm, pa], b["r2m"].at[a, pa], w["to_xm"]) for a in range(2)]

    def pass_p(self):
        w, c, part, b = self.w, self.c, self.part, self.bufs
        xp, xm = w["xp"], w["xm"]
        pa, pb = pl.ds(0, PH), pl.ds(PH, PH)
        for a in range(2):
            self.one_p[a].wait_recv()

            def fn(k, a=a):
                s = pl.ds(k, 48)
                both = b["r1p"][a, s, :].astype(F32) + part[a * 4 + xp, s, :].astype(F32)
                b["r1p"][a, s, :] = both.astype(BF16)

            in_steps(PH, 48, fn)
            self.two.append(c.start(b["r1p"].at[a], b["r2p"].at[a, pa], w["to_xp"]))
            self.one_m[a].wait_recv()

            def fn(k, a=a):
                s, t = pl.ds(k, 48), pl.ds(k + PH, 48)
                both = b["r1m"][a, s, :].astype(F32) + part[a * 4 + xm, t, :].astype(F32)
                b["r1m"][a, s, :] = both.astype(BF16)

            in_steps(PH, 48, fn)
            self.two.append(c.start(b["r1m"].at[a], b["r2m"].at[a, pb], w["to_xm"]))

    def add_q(self, copy, d):
        part, b, yh = self.part, self.bufs, self.w["yh"]
        copy.wait_recv()

        def fn(k):
            s, t = pl.ds(k, 112), pl.ds(k + P_ROWS, 112)
            both = b["rq"][d, s, :].astype(F32) + part[yh * 4 + d, t, :].astype(F32)
            b["rq"][d, s, :] = both.astype(BF16)

        in_steps(Q_ROWS, 112, fn)

    def far_q(self):
        w, c, b, xo = self.w, self.c, self.bufs, self.w["xo"]
        self.add_q(self.q[0], xo)
        self.q1p = c.start(b["rq"].at[xo, pl.ds(0, QH)], b["q1p"], w["to_xp"])
        self.q1m = c.start(b["rq"].at[xo, pl.ds(QH, QH)], b["q1m"], w["to_xm"])

    def near_q(self):
        w, c, b, xp, xm = self.w, self.c, self.bufs, self.w["xp"], self.w["xm"]
        qa, qb = pl.ds(0, QH), pl.ds(QH, QH)
        self.add_q(self.q[1], xp)
        self.q2 = [c.start(b["rq"].at[xp, qb], b["q2p"].at[qb], w["to_xp"])]
        self.add_q(self.q[2], xm)
        self.q2.append(c.start(b["rq"].at[xm, qa], b["q2m"].at[qa], w["to_xm"]))

    def pass_q(self):
        w, c, b, xp, xm = self.w, self.c, self.bufs, self.w["xp"], self.w["xm"]
        self.q1p.wait_recv()
        b["q1p"][...] = (b["q1p"][...].astype(F32) + b["rq"][xp, pl.ds(0, QH), :].astype(F32)).astype(BF16)
        self.q2.append(c.start(b["q1p"], b["q2p"].at[pl.ds(0, QH)], w["to_xp"]))
        self.q1m.wait_recv()
        b["q1m"][...] = (b["q1m"][...].astype(F32) + b["rq"][xm, pl.ds(QH, QH), :].astype(F32)).astype(BF16)
        self.q2.append(c.start(b["q1m"], b["q2m"].at[pl.ds(QH, QH)], w["to_xm"]))

    def sum_p(self, a, s):
        part, b = self.part, self.bufs
        both = b["r2p"][a, s, :].astype(F32) + b["r2m"][a, s, :].astype(F32)
        return both + part[a * 4 + self.w["x"], s, :].astype(F32)

    def cross_p(self):
        w, b, yo, yh = self.w, self.bufs, self.w["yo"], self.w["yh"]
        for copy in self.two:
            copy.wait_recv()

        def fn(k):
            s = pl.ds(k, 48)
            b["r2p"][yo, s, :] = self.sum_p(yo, s).astype(BF16)

        in_steps(P_ROWS, 48, fn)
        self.y = self.c.start(b["r2p"].at[yo], b["ry"], w["to_y"])

        def fn(k):
            s = pl.ds(k, 48)
            self.total[s, :] = self.sum_p(yh, s)

        in_steps(P_ROWS, 48, fn)

    def finish(self, landing):
        w, b, x, total = self.w, self.bufs, self.w["x"], self.total
        self.add_q(self.q[3], x)
        for copy in self.q2:
            copy.wait_recv()

        def fn(k):
            s, t = pl.ds(k, 112), pl.ds(k + P_ROWS, 112)
            both = b["q2p"][s, :].astype(F32) + b["q2m"][s, :].astype(F32)
            total[t, :] = b["rq"][x, s, :].astype(F32) + both

        in_steps(Q_ROWS, 112, fn)
        self.y.wait_recv()

        def fn(k):
            s = pl.ds(k, 48)
            total[s, :] = total[s, :] + b["ry"][s, :].astype(F32)

        in_steps(P_ROWS, 48, fn)

        @pl.loop(0, OWNERS)
        def _(k):
            s = pl.ds(pl.multiple_of(k * HALF, HALF), HALF)
            old = self.base[k, pl.ds(HALF * self.wave, HALF), :]
            new = (old - LEARN * total[s, :]).astype(BF16)
            for u in range(TILE_UNITS):
                self.newv[k * TILE_UNITS + u] = new[u * UNIT : (u + 1) * UNIT]

        landing, owner = landing
        landing = landing.at[self.wave]
        self.shift = [
            self.c.start(self.newv.at[units(0, at, n)], landing.at[units(owner, at, n)], w["to_next"])
            for at, n in ((0, P_ROWS), (P_ROWS, Q_ROWS))
        ]


class Gather:
    def __init__(self, copies, w, wave, vt):
        self.c, self.w, self.vt = copies, w, vt.at[wave]

    def along(self, owner, rows, to):
        ref = self.vt.at[units(owner, *rows)]
        return self.c.start(ref, ref, self.w[to])

    def first(self, shift):
        me = self.w["g"]
        p, q = (0, P_ROWS), (P_ROWS, Q_ROWS)
        shift[0].wait_recv()
        self.py = self.along(me, p, "to_y")
        self.pp = [self.along(me, p, "to_xp")]
        self.pm = [self.along(me, p, "to_xm")]
        shift[1].wait_recv()
        self.qp = self.along(me, q, "to_xp")
        self.qm = self.along(me, q, "to_xm")
        self.rest = [self.along(me, q, "to_y")]

    def across(self):
        w = self.w
        self.py.wait_recv()
        p = (0, P_ROWS)
        self.pp.append(self.along(w["yo"] * 4 + w["x"], p, "to_xp"))
        self.pm.append(self.along(w["yo"] * 4 + w["x"], p, "to_xm"))

    def forward_p(self, k):
        w = self.w
        row = (w["yh"], w["yo"])[k] * 4
        self.pp[k].wait_recv()
        self.rest.append(self.along(row + w["xm"], (0, PH), "to_xp"))
        self.pm[k].wait_recv()
        self.rest.append(self.along(row + w["xp"], (PH, PH), "to_xm"))

    def forward_q(self):
        w = self.w
        row, q = w["yh"] * 4, (P_ROWS, Q_ROWS)
        self.qp.wait_recv()
        self.qf = [self.along(row + w["xm"], (P_ROWS, QH), "to_xp")]
        self.rest.append(self.along(row + w["xm"], q, "to_y"))
        self.qm.wait_recv()
        self.qf.append(self.along(row + w["xp"], (P_ROWS + QH, QH), "to_xm"))
        self.rest.append(self.along(row + w["xp"], q, "to_y"))

    def across_q(self):
        w = self.w
        for copy in self.qf:
            copy.wait_recv()
        self.rest.append(self.along(w["yh"] * 4 + w["xo"], (P_ROWS, Q_ROWS), "to_y"))

    def finish(self):
        for copy in self.rest:
            copy.wait_recv()


def epochs_kernel(
    idx, ratings, mask_in, users_in, items_in, users_out, items_out,
    users, mask, rbuf, err, stage, vown, acc, ub, ubt, vt0, vt1, part,
    r1p, r1m, r2p, r2m, rq, q1p, q1m, q2p, q2m, ry, gsend, grecv, base, total, newv, landing, final,
    rsem, vsem, lsem, send, recv,
):
    w = places()
    copies = Copies(send, recv)
    chunks = SLOTS // GROUP
    stages = stage.shape[0]
    barrier = pltpu.get_barrier_semaphore()
    for peer in PEERS:
        pl.semaphore_signal(barrier, inc=1, device_id=w[peer], device_id_type=MESH)

    def local_copy(src, dst, k):
        copy = pltpu.make_async_copy(src, dst, lsem.at[k])
        copy.start()
        return copy

    users_here = local_copy(users_in, users, 0)

    def items_here(k):
        copy = pltpu.make_async_copy(
            items_in.at[pl.ds(k * OWNERS, OWNERS)], stage.at[k % stages], vsem.at[k]
        )
        copy.start()
        return copy

    arriving = [items_here(k) for k in range(stages)]
    mask_here = local_copy(mask_in, mask, 1)
    own_here = local_copy(items_in.at[pl.ds(w["g"] * OWNERS, OWNERS)], vown, 2)

    def fetch(e, k):
        s = pl.ds(k * GROUP, GROUP)
        return pltpu.make_async_copy(ratings.at[e, s], rbuf.at[s], rsem.at[k])

    def prepare_users(e, first):
        own = jnp.zeros((RANK, RANK), F32)
        for i in range(USER_TILES):
            u = users[pl.ds(i * TILE, TILE), :]
            ub[i] = u.astype(BF16)
            ut = u.T.astype(BF16)
            ubt[0, i], ubt[1, i] = ut[:HALF], ut[HALF:]
            own = own + dot(ut, ub[i])
        own = (own * (GRAM / USER_ROWS) + ridge()).astype(BF16)
        gsend[e, 0] = jnp.where(idx[e, OWNER] == w["g"], own, jnp.zeros_like(own))
        if first:
            pl.semaphore_wait(barrier, len(PEERS))
        return copies.start(gsend.at[e, 0], grecv.at[e, 0], w["to_y"])

    def spread_gram(e, k, copy):
        copy.wait_recv()
        gsend[e, k] = gsend[e, k - 1] + grecv[e, k - 1]
        return copies.start(gsend.at[e, k], grecv.at[e, k], w["to_x1" if k == 1 else "to_xo"])

    def vtile(vt, j):
        first = j * TILE_UNITS
        return jnp.concatenate(
            [vt[wave, first + u] for wave in range(WAVES) for u in range(TILE_UNITS)], axis=0
        )

    def weights(e, t):
        row = mask[e, pl.ds(t, 1), :].astype(F32)
        return jnp.where(t < idx[e, COUNT], row, jnp.zeros_like(row))

    def errors(e, vt, t):
        predicted = dot(ub[idx[e, ROW + t]], vtile(vt, idx[e, COL + t]))
        err[t] = (predicted - rbuf[t].astype(F32)).astype(BF16)

    def item_dot(e, wave, t):
        u = ubt[wave, idx[e, ROW + t]]
        return dot(u * weights(e, t).astype(BF16), err[t])

    def item_add(e, wave, t, add):
        acc[wave, t] = acc[wave, idx[e, PREV_COL + t]] + add

    def item_done(e, wave):
        @pl.loop(0, ITEM_TILES, unroll=4)
        def _(j):
            s = pl.ds(pl.multiple_of(lax.rem(j, OWNERS) * HALF, HALF), HALF)
            part[wave, lax.div(j, OWNERS), s, :] = acc[wave, idx[e, LAST_COL + j]].astype(BF16)

    def first_pass(e, vt):
        fetch(e, 0).wait()
        for q in range(GROUP):
            errors(e, vt, q)

        @pl.loop(0, chunks - 1)
        def _(g):
            adds = [item_dot(e, 0, g * GROUP + q) for q in range(GROUP)]
            fetch(e, g + 1).wait()
            for q in range(GROUP):
                errors(e, vt, (g + 1) * GROUP + q)
            for q in range(GROUP):
                item_add(e, 0, g * GROUP + q, adds[q])

        adds = [item_dot(e, 0, SLOTS - GROUP + q) for q in range(GROUP)]
        for q in range(GROUP):
            item_add(e, 0, SLOTS - GROUP + q, adds[q])
        item_done(e, 0)

    def second_pass(e):
        @pl.loop(0, chunks)
        def _(g):
            adds = [item_dot(e, 1, g * GROUP + q) for q in range(GROUP)]
            for q in range(GROUP):
                item_add(e, 1, g * GROUP + q, adds[q])

        item_done(e, 1)

    def user_pass(e, vt, first, last):
        @pl.loop(first, last)
        def _(g):
            def add_dot(t):
                return dot(vtile(vt, idx[e, COL + t]), err[t], 1, 1) * weights(e, t)

            for h in range(2):
                slots = [g * GROUP + h * (GROUP // 2) + q for q in range(GROUP // 2)]
                adds = [add_dot(t) for t in slots]
                for t, add in zip(slots, adds):
                    before = idx[e, PREV_ROW + t]
                    acc[0, t] = acc[0, before] + add[:HALF]
                    acc[1, t] = acc[1, before] + add[HALF:]

    def item_gram(vt):
        def add(j, gram):
            for q in range(4):
                v = vtile(vt, j * 4 + q)
                gram = gram + dot(v, v, 1, 1)
            return gram

        gram = lax.fori_loop(0, ITEM_TILES // 4, add, jnp.zeros((RANK, RANK), F32))
        return gram * (GRAM / (ITEM_TILES * TILE)) + ridge()

    def user_update(e, pull):
        @pl.loop(0, USER_TILES)
        def _(i):
            s = pl.ds(pl.multiple_of(i * TILE, TILE), TILE)
            u = users[s, :]
            at = idx[e, LAST_ROW + i]
            grad = jnp.concatenate([acc[0, at], acc[1, at]], axis=0)
            users[s, :] = u - LEARN * (grad.T + dot(u, pull, precision=HIGHEST))

    def item_base(e, copy):
        copy.wait_recv()
        pull = (gsend[e, 2] + grecv[e, 2]).astype(F32)

        @pl.loop(0, OWNERS)
        def _(k):
            if e == 0:
                v = vown[k].T
            else:
                v = vtile(vt1, w["g"] * OWNERS + k).astype(F32)
            base[k] = v - LEARN * dot(pull, v, 0, 0, precision=HIGHEST)

    bufs = dict(
        r1p=r1p, r1m=r1m, r2p=r2p, r2m=r2m, rq=rq, q1p=q1p, q1m=q1m, q2p=q2p, q2m=q2m, ry=ry
    )

    def sums(e):
        at = {k: v.at[e] for k, v in bufs.items()}
        return [Sum(copies, w, wave, part, at, base, total, newv) for wave in range(WAVES)]

    users_here.wait()
    gram_copy = prepare_users(0, True)
    zero = jnp.zeros((HALF, TILE), F32)
    acc[0, SLOTS] = zero
    acc[1, SLOTS] = zero
    for k in range(OWNERS):
        arriving[k].wait()

        @pl.loop(0, OWNERS, unroll=2)
        def _(j):
            v = stage[k % stages, j].T.astype(BF16)
            for u in range(TILE_UNITS):
                at = (k * OWNERS + j) * TILE_UNITS + u
                vt0[0, at] = v[u * UNIT : (u + 1) * UNIT]
                vt0[1, at] = v[HALF + u * UNIT : HALF + (u + 1) * UNIT]

        if k + stages < OWNERS:
            arriving.append(items_here(k + stages))
        for c in range(chunks // OWNERS * k, chunks // OWNERS * (k + 1)):
            fetch(0, c).start()
    gram_copy = spread_gram(0, 1, gram_copy)
    mask_here.wait()
    own_here.wait()
    first_pass(0, vt0)
    s0, s1 = sums(0)
    gram_copy = spread_gram(0, 2, gram_copy)
    s0.start()
    for k in range(chunks):
        fetch(1, k).start()
    second_pass(0)
    s0.pass_p()
    s0.far_q()
    s1.start()
    item_base(0, gram_copy)
    s0.near_q()
    s0.pass_q()
    user_pass(0, vt0, 0, 2)
    s0.cross_p()
    s1.pass_p()
    s1.far_q()
    user_pass(0, vt0, 2, 4)
    s0.finish((vt1, w["g"]))
    s1.near_q()
    s1.pass_q()
    g0, g1 = (Gather(copies, w, wave, vt1) for wave in range(WAVES))
    g0.first(s0.shift)
    s1.cross_p()
    user_pass(0, vt0, 4, 6)
    g0.across()
    s1.finish((vt1, w["g"]))
    g0.forward_p(0)
    g0.forward_q()
    g1.first(s1.shift)
    user_pass(0, vt0, 6, 8)
    g0.forward_p(1)
    g0.across_q()
    g1.across()
    pull = item_gram(vt0)
    g1.forward_p(0)
    g1.forward_q()
    user_update(0, pull)
    g1.forward_p(1)
    g1.across_q()
    gram_copy = prepare_users(1, False)
    g0.finish()
    gram_copy = spread_gram(1, 1, gram_copy)
    g1.finish()
    copies.finish()

    first_pass(1, vt1)
    s0, s1 = sums(1)
    gram_copy = spread_gram(1, 2, gram_copy)
    s0.start()
    second_pass(1)
    s0.pass_p()
    s0.far_q()
    s1.start()
    item_base(1, gram_copy)
    s0.near_q()
    s0.pass_q()
    user_pass(1, vt1, 0, 2)
    s0.cross_p()
    s1.pass_p()
    s1.far_q()
    user_pass(1, vt1, 2, 5)
    s0.finish((landing, 0))
    s1.near_q()
    s1.pass_q()
    user_pass(1, vt1, 5, 8)
    s1.cross_p()
    user_update(1, item_gram(vt1))
    users_gone = local_copy(users, users_out, 0)
    s1.finish((landing, 0))
    for copy in s0.shift + s1.shift:
        copy.wait_recv()

    @pl.loop(0, OWNERS)
    def _(k):
        v = vtile(landing, k).astype(F32)
        final[pl.ds(pl.multiple_of(k * TILE, TILE), TILE), :] = v.T

    items_gone = local_copy(final, items_out, 1)
    copies.finish()
    users_gone.wait()
    items_gone.wait()


def epochs(idx, ratings, mask, users, items):
    smem = pl.BlockSpec(memory_space=pltpu.SMEM)
    anywhere = pl.BlockSpec(memory_space=pl.ANY)
    dma = pltpu.SemaphoreType.DMA
    count = ratings.shape[0]

    def wide(*rows):
        return pltpu.VMEM((count, WAVES, *rows, TILE), BF16)

    return pl.pallas_call(
        epochs_kernel,
        out_shape=[jax.ShapeDtypeStruct(users.shape, F32), jax.ShapeDtypeStruct(users.shape, F32)],
        in_specs=[smem, anywhere, anywhere, anywhere, anywhere],
        out_specs=[anywhere, anywhere],
        scratch_shapes=[
            pltpu.VMEM(users.shape, F32),
            pltpu.VMEM(mask.shape, I32),
            pltpu.VMEM((SLOTS, TILE, TILE), BF16),
            pltpu.VMEM((SLOTS, TILE, TILE), BF16),
            pltpu.VMEM((4, OWNERS, TILE, RANK), F32),
            pltpu.VMEM((OWNERS, TILE, RANK), F32),
            pltpu.VMEM((WAVES, SLOTS + 1, HALF, TILE), F32),
            pltpu.VMEM((USER_TILES, TILE, RANK), BF16),
            pltpu.VMEM((WAVES, USER_TILES, HALF, TILE), BF16),
            pltpu.VMEM((WAVES, OWNERS * WAVE_UNITS, UNIT, TILE), BF16),
            pltpu.VMEM((WAVES, OWNERS * WAVE_UNITS, UNIT, TILE), BF16),
            pltpu.VMEM((WAVES, OWNERS, WAVE_ROWS, TILE), BF16),
            wide(2, PH), wide(2, PH), wide(2, P_ROWS), wide(2, P_ROWS),
            wide(4, Q_ROWS), wide(QH), wide(QH), wide(Q_ROWS), wide(Q_ROWS), wide(P_ROWS),
            pltpu.VMEM((count, 3, RANK, RANK), BF16),
            pltpu.VMEM((count, 3, RANK, RANK), BF16),
            pltpu.VMEM((OWNERS, RANK, TILE), F32),
            pltpu.VMEM((WAVES, WAVE_ROWS, TILE), F32),
            pltpu.VMEM((WAVES, WAVE_UNITS, UNIT, TILE), BF16),
            pltpu.VMEM((WAVES, WAVE_UNITS, UNIT, TILE), BF16),
            pltpu.VMEM(users.shape, F32),
            dma((SLOTS // GROUP,)),
            dma((OWNERS,)),
            dma((3,)),
            dma((COPIES,)),
            dma((COPIES,)),
        ],
        compiler_params=pltpu.CompilerParams(
            collective_id=0, has_side_effects=True, vmem_limit_bytes=62 * 2**20
        ),
        name="epochs",
    )(idx, ratings, mask, users, items)


def local(ratings, row_index, col_index, row_mask, counts, owner_list, user_factors, item_factors):
    count = ratings.shape[0]
    idx = table(
        row_index.reshape(count, SLOTS),
        col_index.reshape(count, SLOTS),
        counts.reshape(count),
        owner_list.reshape(count),
    )
    users, items = epochs(
        idx,
        ratings.reshape(count, SLOTS, TILE, TILE),
        row_mask.reshape(count, SLOTS, TILE),
        user_factors,
        item_factors.reshape(ITEM_TILES, TILE, RANK),
    )
    return users, items


def solution(mesh):
    in_specs = (
        P(None, "blk", "grp", None, None, None),
        P(None, "blk", "grp", None),
        P(None, "blk", "grp", None),
        P(None, "blk", "grp", None, None),
        P(None, "blk", "grp"),
        P(None, "blk"),
        P(("blk", "grp"), None),
        P("blk", None),
    )
    out_specs = (P(("blk", "grp"), None), P(("blk", "grp"), None))
    return jax.shard_map(local, mesh=mesh, in_specs=in_specs, out_specs=out_specs, check_vma=False)
```

time: 2020 us -> 147 us (0.07)
  matrix products: 631 us -> 0 us
  waiting for transfers between devices: 537 us -> 0 us
  loops' own time: 515 us -> 0 us
  local copies, waits for them, and re-layouts: 195 us -> 4.52 us
  Pallas kernels: 0 us -> 141 us
  other arithmetic: 111 us -> 0 us
    dot_general x350 -> x0, matrix products: 631 us -> none  [the longest x114 275 us: tile_step(): lax.dot_general(errors, user_part, (((0,), (0,)), ((), ())), preferred_el...]
    another operation x2 -> x0, loops' own time: 515 us -> none  [local(): lax.fori_loop(0, counts[epoch, 0, 0], tile_step, (start_user, start_item))]
    psum x3 -> x0, waiting for transfers between devices: 444 us -> none  [the longest x2 333 us: local(): lax.psum(item_terms.astype(jnp.bfloat16), 'grp').astype(jnp.float32)]
    pallas_call x0 -> x2, Pallas kernels: none -> 141 us  [the longest x1 137 us: epochs(): pl.pallas_call(epochs_kernel, out_shape=[jax.ShapeDtypeStruct(users.shape...]
    dynamic_slice x228 -> x0, local copies, waits for them, and re-layouts: 139 us -> none  [the longest x114 71.1 us: tile_step(): row_tile = rows_in[slot]]
    ppermute x2 -> x0, waiting for transfers between devices: 92.9 us -> none  [passed_along(): lax.ppermute(shard, axis, [(i, (i + by) % length) for i in range(length)])]
    another operation x114 -> x0, other arithmetic: 89.7 us -> none
    convert_element_type x119 -> x0, other arithmetic: 21.2 us -> none  [the longest x2 12.2 us: local(): item_terms.astype(jnp.bfloat16)]
  transfers between devices with their start and end apart: 5 -> 0, of which waited for: 5 -> 0; matrix products, arithmetic and copies ran while one was open for 1% -> 0% of each run, Pallas kernels for 0% -> 0%
where the time goes in v2:
time: 147 us; the launch traced here: 146 us
  Pallas kernels  141 us (96%)
  local copies, waits for them, and re-layouts  4.52 us (3%)
    pallas_call x1, Pallas kernels, epochs(): pl.pallas_call(epochs_kernel, out_shape=[jax.ShapeDtypeStruct(users.shape...  137 us
    unnamed x2, local copies, waits for them, and re-layouts  4.52 us
    pallas_call x1, Pallas kernels, table(): pl.pallas_call(table_kernel, out_shape=jax.ShapeDtypeStruct((rows.shape[0...  4.47 us

profile of v2, /device:TPU:0, one launch (start us, length us, event | category | flops | bytes accessed | tf_op | source)
XLA Modules:
  0.0 146.5 jit_solution(16840943994871883782)
XLA Ops:
  0.6 4.5 %table.1.idx = s32[2,384]{1,0:T(2,128)} custom-call(s32[2,64]{1,0:T(2,128)} %bitcast.10, s32[2,64]{1,0:T(2,128)} %bitcast.11, s32[2]{0:T(128)} %bitcast.12, s32[2]{0:T(128)} %bitcast.13), custom_call_target="tpu_custom_call" | custom-call | tf_op jit(solution)/shard_map/table/pallas_call | solution.py:85
  5.1 136.8 %epochs.1 = (f32[2048,128]{1,0:T(8,128)}, f32[2048,128]{1,0:T(8,128)}) custom-call(s32[2,384]{1,0:T(2,128)} %table.1.idx, bf16[2,64,256,256]{3,2,1,0:T(8,128)(2,1)} %bitcast.7, s32[2,64,256]{2,1,0:T(8,128)} %bitcast.9, f32[2048,128]{1,0:T(8,128)} %users_in.1, f32[64,256,128]{2,1,0:T(8,128)} %bitcast.8), custom_call_target="tpu_custom_call" | custom-call | tf_op jit(solution)/shard_map/epochs/pallas_call | solution.py:617
  141.9 2.3 %copy.12 = f32[2048,128]{1,0:T(8,128)} copy(f32[2048,128]{1,0:T(8,128)} %get-tuple-element.4) | data formatting | bytes 2097152
  144.2 2.3 %copy.13 = f32[2048,128]{1,0:T(8,128)} copy(f32[2048,128]{1,0:T(8,128)} %get-tuple-element.5) | data formatting | bytes 2097152

commit v3 on v2

--- a/solution.py
+++ b/solution.py
@@ -35,7 +35,7 @@
     return pl.ds(owner * WAVE_UNITS + start // UNIT, rows // UNIT)
 
 
-PREV_COL, PREV_ROW, COL, ROW, LAST_COL, LAST_ROW, COUNT, OWNER, TABLE = 0, 64, 128, 192, 256, 320, 328, 329, 384
+PREV_COL, PREV_ROW, LAST_COL, LAST_ROW, LISTS = 0, 1, 2, 3, 4
 
 F32, BF16, I32 = jnp.float32, jnp.bfloat16, jnp.int32
 MESH = pl.DeviceIdType.MESH
@@ -52,43 +52,6 @@
     row = lax.broadcasted_iota(I32, (RANK, RANK), 0)
     col = lax.broadcasted_iota(I32, (RANK, RANK), 1)
     return jnp.where(row == col, RIDGE, 0.0).astype(F32)
-
-
-def table_kernel(rows, cols, counts, owner, out):
-    for e in range(rows.shape[0]):
-        n = counts[e]
-
-        @pl.loop(0, SLOTS, unroll=8)
-        def _(t):
-            out[e, PREV_COL + t] = SLOTS
-            out[e, PREV_ROW + t] = SLOTS
-            out[e, LAST_COL + t] = SLOTS
-            out[e, COL + t] = cols[e, t]
-            out[e, ROW + t] = rows[e, t]
-
-        for i in range(USER_TILES):
-            out[e, LAST_ROW + i] = SLOTS
-        out[e, COUNT] = n
-        out[e, OWNER] = owner[e]
-
-        @pl.loop(0, n)
-        def _(t):
-            c, r = cols[e, t], rows[e, t]
-            out[e, PREV_COL + t] = out[e, LAST_COL + c]
-            out[e, LAST_COL + c] = t
-            out[e, PREV_ROW + t] = out[e, LAST_ROW + r]
-            out[e, LAST_ROW + r] = t
-
-
-def table(rows, cols, counts, owner):
-    smem = pl.BlockSpec(memory_space=pltpu.SMEM)
-    return pl.pallas_call(
-        table_kernel,
-        out_shape=jax.ShapeDtypeStruct((rows.shape[0], TABLE), I32),
-        in_specs=[smem] * 4,
-        out_specs=smem,
-        name="table",
-    )(rows, cols, counts, owner)
 
 
 def places():
@@ -142,6 +105,15 @@
 
 COPIES = 160
 
+ORDER_0 = (
+    "s0", "B", "p0", "f0", "s1", "I", "n0", "q0", "U", "c0", "p1", "f1", "F0", "a0", "n1", "q1",
+    "U", "x0", "c1", "k0", "r0", "U", "F1", "l0", "a1", "z0", "U", "x1", "k1", "r1", "V", "l1", "z1",
+)
+ORDER_1 = (
+    "s0", "B", "p0", "f0", "s1", "I", "n0", "q0", "U", "c0", "p1", "f1", "U", "F0", "n1", "q1", "U", "U", "c1", "V", "O",
+    "F1",
+)
+
 
 class Sum:
     def __init__(self, copies, w, wave, part, bufs, base, total, newv):
@@ -154,20 +126,26 @@
         w, c, part, b = self.w, self.c, self.part, self.bufs
         xp, xm, xo, yo = w["xp"], w["xm"], w["xo"], w["yo"]
         pa, pb, q = pl.ds(0, PH), pl.ds(PH, PH), pl.ds(P_ROWS, Q_ROWS)
-        self.one_p = [c.start(part.at[a * 4 + xo, pa], b["r1p"].at[a], w["to_xp"]) for a in range(2)]
-        self.one_m = [c.start(part.at[a * 4 + xo, pb], b["r1m"].at[a], w["to_xm"]) for a in range(2)]
+        self.rows = rows = (yo, w["yh"])
+        self.one_p, self.one_m = [], []
+        for a in rows:
+            self.one_p.append(c.start(part.at[a * 4 + xo, pa], b["r1p"].at[a], w["to_xp"]))
+            self.one_m.append(c.start(part.at[a * 4 + xo, pb], b["r1m"].at[a], w["to_xm"]))
         self.q = [
             c.start(part.at[yo * 4 + d, q], b["rq"].at[d], w["to_y"]) for d in (xo, xp, xm, w["x"])
         ]
-        self.two = [c.start(part.at[a * 4 + xp, pb], b["r2p"].at[a, pb], w["to_xp"]) for a in range(2)]
-        self.two += [c.start(part.at[a * 4 + xm, pa], b["r2m"].at[a, pa], w["to_xm"]) for a in range(2)]
+        self.two = []
+        for a in rows:
+            to_p = c.start(part.at[a * 4 + xp, pb], b["r2p"].at[a, pb], w["to_xp"])
+            to_m = c.start(part.at[a * 4 + xm, pa], b["r2m"].at[a, pa], w["to_xm"])
+            self.two.append([to_p, to_m])
 
     def pass_p(self):
         w, c, part, b = self.w, self.c, self.part, self.bufs
         xp, xm = w["xp"], w["xm"]
         pa, pb = pl.ds(0, PH), pl.ds(PH, PH)
-        for a in range(2):
-            self.one_p[a].wait_recv()
+        for k, a in enumerate(self.rows):
+            self.one_p[k].wait_recv()
 
             def fn(k, a=a):
                 s = pl.ds(k, 48)
@@ -175,8 +153,8 @@
                 b["r1p"][a, s, :] = both.astype(BF16)
 
             in_steps(PH, 48, fn)
-            self.two.append(c.start(b["r1p"].at[a], b["r2p"].at[a, pa], w["to_xp"]))
-            self.one_m[a].wait_recv()
+            self.two[k].append(c.start(b["r1p"].at[a], b["r2p"].at[a, pa], w["to_xp"]))
+            self.one_m[k].wait_recv()
 
             def fn(k, a=a):
                 s, t = pl.ds(k, 48), pl.ds(k + PH, 48)
@@ -184,7 +162,7 @@
                 b["r1m"][a, s, :] = both.astype(BF16)
 
             in_steps(PH, 48, fn)
-            self.two.append(c.start(b["r1m"].at[a], b["r2m"].at[a, pb], w["to_xm"]))
+            self.two[k].append(c.start(b["r1m"].at[a], b["r2m"].at[a, pb], w["to_xm"]))
 
     def add_q(self, copy, d):
         part, b, yh = self.part, self.bufs, self.w["yh"]
@@ -227,7 +205,7 @@
 
     def cross_p(self):
         w, b, yo, yh = self.w, self.bufs, self.w["yo"], self.w["yh"]
-        for copy in self.two:
+        for copy in self.two[0]:
             copy.wait_recv()
 
         def fn(k):
@@ -236,6 +214,8 @@
 
         in_steps(P_ROWS, 48, fn)
         self.y = self.c.start(b["r2p"].at[yo], b["ry"], w["to_y"])
+        for copy in self.two[1]:
+            copy.wait_recv()
 
         def fn(k):
             s = pl.ds(k, 48)
@@ -287,8 +267,8 @@
         ref = self.vt.at[units(owner, *rows)]
         return self.c.start(ref, ref, self.w[to])
 
-    def first(self, shift):
-        me = self.w["g"]
+    def first(self, one):
+        shift, me = one.shift, self.w["g"]
         p, q = (0, P_ROWS), (P_ROWS, Q_ROWS)
         shift[0].wait_recv()
         self.py = self.along(me, p, "to_y")
@@ -335,9 +315,23 @@
             copy.wait_recv()
 
 
+def chains(keys, count):
+    lane = lax.broadcasted_iota(I32, (SLOTS, SLOTS), 1)
+    slot = lax.broadcasted_iota(I32, (SLOTS, SLOTS), 0)
+    across = jnp.broadcast_to(keys, (SLOTS, SLOTS))
+    down = jnp.sum(jnp.where(lane == slot, across, 0), axis=1, keepdims=True)
+    live = slot < count
+
+    def latest(where):
+        found = jnp.max(jnp.where(where & live, slot, -1), axis=0, keepdims=True)
+        return jnp.where(found < 0, SLOTS, found)
+
+    return latest((down == across) & (slot < lane)), latest(down == lane)
+
+
 def epochs_kernel(
-    idx, ratings, mask_in, users_in, items_in, users_out, items_out,
-    users, mask, rbuf, err, stage, vown, acc, ub, ubt, vt0, vt1, part,
+    counts, owner, rows_in, cols_in, ratings, mask_in, users_in, items_in, users_out, items_out,
+    rows_v, cols_v, rows_s, cols_s, lists, idx, users, mask, rbuf, err, stage, vown, acc, ub, ubt, vt0, vt1, part,
     r1p, r1m, r2p, r2m, rq, q1p, q1m, q2p, q2m, ry, gsend, grecv, base, total, newv, landing, final,
     rsem, vsem, lsem, send, recv,
 ):
@@ -354,6 +348,10 @@
         copy.start()
         return copy
 
+    lists_in = [
+        local_copy(a, b, 3 + k)
+        for k, (a, b) in enumerate(((cols_in, cols_v), (rows_in, rows_v), (cols_in, cols_s), (rows_in, rows_s)))
+    ]
     users_here = local_copy(users_in, users, 0)
 
     def items_here(k):
@@ -380,7 +378,7 @@
             ubt[0, i], ubt[1, i] = ut[:HALF], ut[HALF:]
             own = own + dot(ut, ub[i])
         own = (own * (GRAM / USER_ROWS) + ridge()).astype(BF16)
-        gsend[e, 0] = jnp.where(idx[e, OWNER] == w["g"], own, jnp.zeros_like(own))
+        gsend[e, 0] = jnp.where(owner[e] == w["g"], own, jnp.zeros_like(own))
         if first:
             pl.semaphore_wait(barrier, len(PEERS))
         return copies.start(gsend.at[e, 0], grecv.at[e, 0], w["to_y"])
@@ -398,24 +396,24 @@
 
     def weights(e, t):
         row = mask[e, pl.ds(t, 1), :].astype(F32)
-        return jnp.where(t < idx[e, COUNT], row, jnp.zeros_like(row))
+        return jnp.where(t < counts[e], row, jnp.zeros_like(row))
 
     def errors(e, vt, t):
-        predicted = dot(ub[idx[e, ROW + t]], vtile(vt, idx[e, COL + t]))
+        predicted = dot(ub[rows_s[e, t]], vtile(vt, cols_s[e, t]))
         err[t] = (predicted - rbuf[t].astype(F32)).astype(BF16)
 
     def item_dot(e, wave, t):
-        u = ubt[wave, idx[e, ROW + t]]
+        u = ubt[wave, rows_s[e, t]]
         return dot(u * weights(e, t).astype(BF16), err[t])
 
     def item_add(e, wave, t, add):
-        acc[wave, t] = acc[wave, idx[e, PREV_COL + t]] + add
+        acc[wave, t] = acc[wave, idx[e * LISTS + PREV_COL, t]] + add
 
     def item_done(e, wave):
         @pl.loop(0, ITEM_TILES, unroll=4)
         def _(j):
             s = pl.ds(pl.multiple_of(lax.rem(j, OWNERS) * HALF, HALF), HALF)
-            part[wave, lax.div(j, OWNERS), s, :] = acc[wave, idx[e, LAST_COL + j]].astype(BF16)
+            part[wave, lax.div(j, OWNERS), s, :] = acc[wave, idx[e * LISTS + LAST_COL, j]].astype(BF16)
 
     def first_pass(e, vt):
         fetch(e, 0).wait()
@@ -449,13 +447,13 @@
         @pl.loop(first, last)
         def _(g):
             def add_dot(t):
-                return dot(vtile(vt, idx[e, COL + t]), err[t], 1, 1) * weights(e, t)
+                return dot(vtile(vt, cols_s[e, t]), err[t], 1, 1) * weights(e, t)
 
             for h in range(2):
                 slots = [g * GROUP + h * (GROUP // 2) + q for q in range(GROUP // 2)]
                 adds = [add_dot(t) for t in slots]
                 for t, add in zip(slots, adds):
-                    before = idx[e, PREV_ROW + t]
+                    before = idx[e * LISTS + PREV_ROW, t]
                     acc[0, t] = acc[0, before] + add[:HALF]
                     acc[1, t] = acc[1, before] + add[HALF:]
 
@@ -474,7 +472,7 @@
         def _(i):
             s = pl.ds(pl.multiple_of(i * TILE, TILE), TILE)
             u = users[s, :]
-            at = idx[e, LAST_ROW + i]
+            at = idx[e * LISTS + LAST_ROW, i]
             grad = jnp.concatenate([acc[0, at], acc[1, at]], axis=0)
             users[s, :] = u - LEARN * (grad.T + dot(u, pull, precision=HIGHEST))
 
@@ -498,6 +496,15 @@
         at = {k: v.at[e] for k, v in bufs.items()}
         return [Sum(copies, w, wave, part, at, base, total, newv) for wave in range(WAVES)]
 
+    for copy in lists_in:
+        copy.wait()
+    for e in range(ratings.shape[0]):
+        for k, keys in enumerate((cols_v, rows_v)):
+            prev, final_slot = chains(keys[e : e + 1, :], counts[e])
+            at = e * LISTS + k
+            lists[at : at + 1, 0:SLOTS] = prev
+            lists[at + 2 : at + 3, 0:SLOTS] = final_slot
+    lists_out = local_copy(lists, idx, 7)
     users_here.wait()
     gram_copy = prepare_users(0, True)
     zero = jnp.zeros((HALF, TILE), F32)
@@ -520,77 +527,59 @@
             fetch(0, c).start()
     gram_copy = spread_gram(0, 1, gram_copy)
     mask_here.wait()
+    lists_out.wait()
     own_here.wait()
+
+    def steps(e, vt, landing, gather):
+        waves = sums(e)
+        table = {}
+        for k, one in enumerate(waves):
+            table.update({
+                "s%d" % k: one.start, "p%d" % k: one.pass_p, "f%d" % k: one.far_q, "n%d" % k: one.near_q,
+                "q%d" % k: one.pass_q, "c%d" % k: one.cross_p,
+                "F%d" % k: functools.partial(one.finish, landing),
+            })
+            if gather is not None:
+                to = Gather(copies, w, k, gather)
+                table.update({
+                    "a%d" % k: functools.partial(to.first, one), "x%d" % k: to.across,
+                    "k%d" % k: functools.partial(to.forward_p, 0), "r%d" % k: to.forward_q,
+                    "l%d" % k: functools.partial(to.forward_p, 1), "z%d" % k: to.across_q, "e%d" % k: to.finish,
+                })
+        done = [0]
+
+        def some_users():
+            user_pass(e, vt, done[0], done[0] + 2)
+            done[0] += 2
+
+        table.update(B=functools.partial(second_pass, e), U=some_users)
+        table["V"] = lambda: user_update(e, item_gram(vt))
+        return waves, table
+
     first_pass(0, vt0)
-    s0, s1 = sums(0)
     gram_copy = spread_gram(0, 2, gram_copy)
-    s0.start()
+    waves, table = steps(0, vt0, (vt1, w["g"]), vt1)
+    table["I"] = lambda: item_base(0, gram_copy)
     for k in range(chunks):
         fetch(1, k).start()
-    second_pass(0)
-    s0.pass_p()
-    s0.far_q()
-    s1.start()
-    item_base(0, gram_copy)
-    s0.near_q()
-    s0.pass_q()
-    user_pass(0, vt0, 0, 2)
-    s0.cross_p()
-    s1.pass_p()
-    s1.far_q()
-    user_pass(0, vt0, 2, 4)
-    s0.finish((vt1, w["g"]))
-    s1.near_q()
-    s1.pass_q()
-    g0, g1 = (Gather(copies, w, wave, vt1) for wave in range(WAVES))
-    g0.first(s0.shift)
-    s1.cross_p()
-    user_pass(0, vt0, 4, 6)
-    g0.across()
-    s1.finish((vt1, w["g"]))
-    g0.forward_p(0)
-    g0.forward_q()
-    g1.first(s1.shift)
-    user_pass(0, vt0, 6, 8)
-    g0.forward_p(1)
-    g0.across_q()
-    g1.across()
-    pull = item_gram(vt0)
-    g1.forward_p(0)
-    g1.forward_q()
-    user_update(0, pull)
-    g1.forward_p(1)
-    g1.across_q()
+    for step in ORDER_0:
+        table[step]()
     gram_copy = prepare_users(1, False)
-    g0.finish()
+    table["e0"]()
     gram_copy = spread_gram(1, 1, gram_copy)
-    g1.finish()
+    table["e1"]()
     copies.finish()
 
     first_pass(1, vt1)
-    s0, s1 = sums(1)
     gram_copy = spread_gram(1, 2, gram_copy)
-    s0.start()
-    second_pass(1)
-    s0.pass_p()
-    s0.far_q()
-    s1.start()
-    item_base(1, gram_copy)
-    s0.near_q()
-    s0.pass_q()
-    user_pass(1, vt1, 0, 2)
-    s0.cross_p()
-    s1.pass_p()
-    s1.far_q()
-    user_pass(1, vt1, 2, 5)
-    s0.finish((landing, 0))
-    s1.near_q()
-    s1.pass_q()
-    user_pass(1, vt1, 5, 8)
-    s1.cross_p()
-    user_update(1, item_gram(vt1))
-    users_gone = local_copy(users, users_out, 0)
-    s1.finish((landing, 0))
+    waves, table = steps(1, vt1, (landing, 0), None)
+    table["I"] = lambda: item_base(1, gram_copy)
+    sent = []
+    table["O"] = lambda: sent.append(local_copy(users, users_out, 0))
+    for step in ORDER_1:
+        table[step]()
+    users_gone = sent[0]
+    s0, s1 = waves
     for copy in s0.shift + s1.shift:
         copy.wait_recv()
 
@@ -605,7 +594,7 @@
     items_gone.wait()
 
 
-def epochs(idx, ratings, mask, users, items):
+def epochs(counts, owner, rows, cols, ratings, mask, users, items):
     smem = pl.BlockSpec(memory_space=pltpu.SMEM)
     anywhere = pl.BlockSpec(memory_space=pl.ANY)
     dma = pltpu.SemaphoreType.DMA
@@ -617,9 +606,15 @@
     return pl.pallas_call(
         epochs_kernel,
         out_shape=[jax.ShapeDtypeStruct(users.shape, F32), jax.ShapeDtypeStruct(users.shape, F32)],
-        in_specs=[smem, anywhere, anywhere, anywhere, anywhere],
+        in_specs=[smem] * 2 + [anywhere] * 6,
         out_specs=[anywhere, anywhere],
         scratch_shapes=[
+            pltpu.VMEM(rows.shape, I32),
+            pltpu.VMEM(cols.shape, I32),
+            pltpu.SMEM(rows.shape, I32),
+            pltpu.SMEM(cols.shape, I32),
+            pltpu.VMEM((count * LISTS, 128), I32),
+            pltpu.SMEM((count * LISTS, 128), I32),
             pltpu.VMEM(users.shape, F32),
             pltpu.VMEM(mask.shape, I32),
             pltpu.VMEM((SLOTS, TILE, TILE), BF16),
@@ -643,7 +638,7 @@
             pltpu.VMEM(users.shape, F32),
             dma((SLOTS // GROUP,)),
             dma((OWNERS,)),
-            dma((3,)),
+            dma((8,)),
             dma((COPIES,)),
             dma((COPIES,)),
         ],
@@ -651,25 +646,64 @@
             collective_id=0, has_side_effects=True, vmem_limit_bytes=62 * 2**20
         ),
         name="epochs",
-    )(idx, ratings, mask, users, items)
+    )(counts, owner, rows, cols, ratings, mask, users, items)
+
+
+PIECES = 4
+
+
+def settle_kernel(a, b, a_out, b_out, a_here, b_here, come, go):
+    rows = a.shape[0] // PIECES
+    moves = []
+    for src, here, dst in ((a, a_here, a_out), (b, b_here, b_out)):
+        for k in range(PIECES):
+            s, n = pl.ds(k * rows, rows), len(moves)
+            moves.append(
+                (
+                    pltpu.make_async_copy(src.at[s], here.at[s], come.at[n]),
+                    pltpu.make_async_copy(here.at[s], dst.at[s], go.at[n]),
+                )
+            )
+    for first, _ in moves:
+        first.start()
+    for first, second in moves:
+        first.wait()
+        second.start()
+    for _, second in moves:
+        second.wait()
+
+
+def settled(a, b):
+    anywhere = pl.BlockSpec(memory_space=pl.ANY)
+    dma = pltpu.SemaphoreType.DMA
+    return pl.pallas_call(
+        settle_kernel,
+        out_shape=[jax.ShapeDtypeStruct(a.shape, a.dtype), jax.ShapeDtypeStruct(b.shape, b.dtype)],
+        in_specs=[anywhere] * 2,
+        out_specs=[anywhere] * 2,
+        scratch_shapes=[
+            pltpu.VMEM(a.shape, a.dtype),
+            pltpu.VMEM(b.shape, b.dtype),
+            dma((2 * PIECES,)),
+            dma((2 * PIECES,)),
+        ],
+        name="settle",
+    )(a, b)
 
 
 def local(ratings, row_index, col_index, row_mask, counts, owner_list, user_factors, item_factors):
     count = ratings.shape[0]
-    idx = table(
+    users, items = epochs(
+        counts.reshape(count),
+        owner_list.reshape(count),
         row_index.reshape(count, SLOTS),
         col_index.reshape(count, SLOTS),
-        counts.reshape(count),
-        owner_list.reshape(count),
-    )
-    users, items = epochs(
-        idx,
         ratings.reshape(count, SLOTS, TILE, TILE),
         row_mask.reshape(count, SLOTS, TILE),
         user_factors,
         item_factors.reshape(ITEM_TILES, TILE, RANK),
     )
-    return users, items
+    return settled(users, items)
 
 
 def solution(mesh):

time: 147 us -> 135 us (0.918)
  Pallas kernels: 141 us -> 134 us
  local copies, waits for them, and re-layouts: 4.52 us -> 0 us
    pallas_call x1, Pallas kernels: 137 us -> 131 us  [epochs(): pl.pallas_call(epochs_kernel, out_shape=[jax.ShapeDtypeStruct(users.shape...]
    unnamed x2 -> x0, local copies, waits for them, and re-layouts: 4.52 us -> none
    pallas_call x1, Pallas kernels: 4.47 us -> 2.4 us  [settled(): pl.pallas_call(settle_kernel, out_shape=[jax.ShapeDtypeStruct(a.shape, a....]
where the time goes in v3:
time: 135 us; the launch traced here: 134 us
  Pallas kernels  134 us (99%)
    pallas_call x1, Pallas kernels, epochs(): pl.pallas_call(epochs_kernel, out_shape=[jax.ShapeDtypeStruct(users.shape...  131 us

profile of v3, /device:TPU:0, one launch (start us, length us, event | category | flops | bytes accessed | tf_op | source)
XLA Modules:
  0.0 134.1 jit_solution(18355793710368317)
XLA Ops:
  0.6 131.1 %epochs.1 = (f32[2048,128]{1,0:T(8,128)}, f32[2048,128]{1,0:T(8,128)}) custom-call(s32[2]{0:T(128)} %bitcast.12, s32[2]{0:T(128)} %bitcast.13, s32[2,64]{1,0:T(2,128)} %bitcast.10, s32[2,64]{1,0:T(2,128)} %bitcast.11, bf16[2,64,256,256]{3,2,1,0:T(8,128)(2,1)} %bitcast.7, s32[2,64,256]{2,1,0:T(8,128)} %bitcast.9, f32[2048,128]{1,0:T(8,128)} %users_in.1, ...), custom_call_target="tpu_custom_call" | custom-call | tf_op jit(solution)/shard_map/epochs/pallas_call | solution.py:606
  131.7 2.4 %settle.1 = (f32[2048,128]{1,0:T(8,128)}, f32[2048,128]{1,0:T(8,128)}) custom-call(f32[2048,128]{1,0:T(8,128)} %get-tuple-element.4.a, f32[2048,128]{1,0:T(8,128)} %get-tuple-element.5.b), custom_call_target="tpu_custom_call" | custom-call | tf_op jit(solution)/shard_map/settle/pallas_call | solution.py:679

commit v4 on v3

--- a/solution.py
+++ b/solution.py
@@ -106,12 +106,14 @@
 COPIES = 160
 
 ORDER_0 = (
-    "s0", "B", "p0", "f0", "s1", "I", "n0", "q0", "U", "c0", "p1", "f1", "F0", "a0", "n1", "q1",
-    "U", "x0", "c1", "k0", "r0", "U", "F1", "l0", "a1", "z0", "U", "x1", "k1", "r1", "V", "l1", "z1",
+    "s0", "g0", "t0", "B", "U", "p0", "s1", "c0", "P0", "v0", "U", "f0", "u0", "g1", "I", "n0",
+    "p1", "q0", "u1", "t1", "v1", "C0", "F0", "f1", "P1", "c1", "n1", "q1", "a0", "U", "b0", "C1",
+    "F1", "x0", "U", "a1", "r0", "b1", "x1", "z0", "V", "l0", "r1", "l1", "z1", "k0", "k1",
 )
 ORDER_1 = (
-    "s0", "B", "p0", "f0", "s1", "I", "n0", "q0", "U", "c0", "p1", "f1", "U", "F0", "n1", "q1", "U", "U", "c1", "V", "O",
-    "F1",
+    "s0", "g0", "B", "s1", "p0", "t0", "g1", "u0", "P0", "f0", "u1", "U", "t1", "U", "I", "c0",
+    "v1", "v0", "U", "n0", "p1", "U", "f1", "q0", "n1", "P1", "c1", "C0", "q1", "F0", "C1", "F1",
+    "V", "O",
 )
 
 
@@ -123,46 +125,48 @@
         self.base, self.total, self.newv = base, total.at[wave], newv.at[wave]
 
     def start(self):
-        w, c, part, b = self.w, self.c, self.part, self.bufs
-        xp, xm, xo, yo = w["xp"], w["xm"], w["xo"], w["yo"]
-        pa, pb, q = pl.ds(0, PH), pl.ds(PH, PH), pl.ds(P_ROWS, Q_ROWS)
-        self.rows = rows = (yo, w["yh"])
-        self.one_p, self.one_m = [], []
-        for a in rows:
-            self.one_p.append(c.start(part.at[a * 4 + xo, pa], b["r1p"].at[a], w["to_xp"]))
-            self.one_m.append(c.start(part.at[a * 4 + xo, pb], b["r1m"].at[a], w["to_xm"]))
-        self.q = [
-            c.start(part.at[yo * 4 + d, q], b["rq"].at[d], w["to_y"]) for d in (xo, xp, xm, w["x"])
-        ]
-        self.two = []
-        for a in rows:
-            to_p = c.start(part.at[a * 4 + xp, pb], b["r2p"].at[a, pb], w["to_xp"])
-            to_m = c.start(part.at[a * 4 + xm, pa], b["r2m"].at[a, pa], w["to_xm"])
-            self.two.append([to_p, to_m])
-
-    def pass_p(self):
-        w, c, part, b = self.w, self.c, self.part, self.bufs
+        w, c, part, b, xo = self.w, self.c, self.part, self.bufs, self.w["xo"]
+        self.rows = (w["yo"], w["yh"])
+        self.one_p, self.one_m, self.q, self.two = [], [], {}, [[], []]
+        for a in self.rows:
+            self.one_p.append(c.start(part.at[a * 4 + xo, pl.ds(0, PH)], b["r1p"].at[a], w["to_xp"]))
+            self.one_m.append(c.start(part.at[a * 4 + xo, pl.ds(PH, PH)], b["r1m"].at[a], w["to_xm"]))
+        self.send_q("xo")
+
+    def send_q(self, *names):
+        w = self.w
+        for name in names:
+            self.q[name] = self.c.start(
+                self.part.at[w["yo"] * 4 + w[name], pl.ds(P_ROWS, Q_ROWS)], self.bufs["rq"].at[w[name]], w["to_y"]
+            )
+
+    def send_p(self, k):
+        w, c, part, b, a = self.w, self.c, self.part, self.bufs, self.rows[k]
+        pa, pb = pl.ds(0, PH), pl.ds(PH, PH)
+        self.two[k].append(c.start(part.at[a * 4 + w["xp"], pb], b["r2p"].at[a, pb], w["to_xp"]))
+        self.two[k].append(c.start(part.at[a * 4 + w["xm"], pa], b["r2m"].at[a, pa], w["to_xm"]))
+
+    def pass_p(self, k):
+        w, c, part, b, a = self.w, self.c, self.part, self.bufs, self.rows[k]
         xp, xm = w["xp"], w["xm"]
-        pa, pb = pl.ds(0, PH), pl.ds(PH, PH)
-        for k, a in enumerate(self.rows):
-            self.one_p[k].wait_recv()
-
-            def fn(k, a=a):
-                s = pl.ds(k, 48)
-                both = b["r1p"][a, s, :].astype(F32) + part[a * 4 + xp, s, :].astype(F32)
-                b["r1p"][a, s, :] = both.astype(BF16)
-
-            in_steps(PH, 48, fn)
-            self.two[k].append(c.start(b["r1p"].at[a], b["r2p"].at[a, pa], w["to_xp"]))
-            self.one_m[k].wait_recv()
-
-            def fn(k, a=a):
-                s, t = pl.ds(k, 48), pl.ds(k + PH, 48)
-                both = b["r1m"][a, s, :].astype(F32) + part[a * 4 + xm, t, :].astype(F32)
-                b["r1m"][a, s, :] = both.astype(BF16)
-
-            in_steps(PH, 48, fn)
-            self.two[k].append(c.start(b["r1m"].at[a], b["r2m"].at[a, pb], w["to_xm"]))
+        self.one_p[k].wait_recv()
+
+        def fn(at):
+            s = pl.ds(at, 48)
+            both = b["r1p"][a, s, :].astype(F32) + part[a * 4 + xp, s, :].astype(F32)
+            b["r1p"][a, s, :] = both.astype(BF16)
+
+        in_steps(PH, 48, fn)
+        self.two[k].append(c.start(b["r1p"].at[a], b["r2p"].at[a, pl.ds(0, PH)], w["to_xp"]))
+        self.one_m[k].wait_recv()
+
+        def fn(at):
+            s, t = pl.ds(at, 48), pl.ds(at + PH, 48)
+            both = b["r1m"][a, s, :].astype(F32) + part[a * 4 + xm, t, :].astype(F32)
+            b["r1m"][a, s, :] = both.astype(BF16)
+
+        in_steps(PH, 48, fn)
+        self.two[k].append(c.start(b["r1m"].at[a], b["r2m"].at[a, pl.ds(PH, PH)], w["to_xm"]))
 
     def add_q(self, copy, d):
         part, b, yh = self.part, self.bufs, self.w["yh"]
@@ -177,16 +181,16 @@
 
     def far_q(self):
         w, c, b, xo = self.w, self.c, self.bufs, self.w["xo"]
-        self.add_q(self.q[0], xo)
+        self.add_q(self.q["xo"], xo)
         self.q1p = c.start(b["rq"].at[xo, pl.ds(0, QH)], b["q1p"], w["to_xp"])
         self.q1m = c.start(b["rq"].at[xo, pl.ds(QH, QH)], b["q1m"], w["to_xm"])
 
     def near_q(self):
         w, c, b, xp, xm = self.w, self.c, self.bufs, self.w["xp"], self.w["xm"]
         qa, qb = pl.ds(0, QH), pl.ds(QH, QH)
-        self.add_q(self.q[1], xp)
+        self.add_q(self.q["xp"], xp)
         self.q2 = [c.start(b["rq"].at[xp, qb], b["q2p"].at[qb], w["to_xp"])]
-        self.add_q(self.q[2], xm)
+        self.add_q(self.q["xm"], xm)
         self.q2.append(c.start(b["rq"].at[xm, qa], b["q2m"].at[qa], w["to_xm"]))
 
     def pass_q(self):
@@ -204,7 +208,7 @@
         return both + part[a * 4 + self.w["x"], s, :].astype(F32)
 
     def cross_p(self):
-        w, b, yo, yh = self.w, self.bufs, self.w["yo"], self.w["yh"]
+        w, b, yo = self.w, self.bufs, self.w["yo"]
         for copy in self.two[0]:
             copy.wait_recv()
 
@@ -214,6 +218,9 @@
 
         in_steps(P_ROWS, 48, fn)
         self.y = self.c.start(b["r2p"].at[yo], b["ry"], w["to_y"])
+
+    def keep_p(self):
+        yh = self.w["yh"]
         for copy in self.two[1]:
             copy.wait_recv()
 
@@ -225,7 +232,7 @@
 
     def finish(self, landing):
         w, b, x, total = self.w, self.bufs, self.w["x"], self.total
-        self.add_q(self.q[3], x)
+        self.add_q(self.q["x"], x)
         for copy in self.q2:
             copy.wait_recv()
 
@@ -269,12 +276,15 @@
 
     def first(self, one):
         shift, me = one.shift, self.w["g"]
-        p, q = (0, P_ROWS), (P_ROWS, Q_ROWS)
+        p = (0, P_ROWS)
         shift[0].wait_recv()
         self.py = self.along(me, p, "to_y")
         self.pp = [self.along(me, p, "to_xp")]
         self.pm = [self.along(me, p, "to_xm")]
-        shift[1].wait_recv()
+
+    def first_q(self, one):
+        me, q = self.w["g"], (P_ROWS, Q_ROWS)
+        one.shift[1].wait_recv()
         self.qp = self.along(me, q, "to_xp")
         self.qm = self.along(me, q, "to_xm")
         self.rest = [self.along(me, q, "to_y")]
@@ -535,14 +545,17 @@
         table = {}
         for k, one in enumerate(waves):
             table.update({
-                "s%d" % k: one.start, "p%d" % k: one.pass_p, "f%d" % k: one.far_q, "n%d" % k: one.near_q,
-                "q%d" % k: one.pass_q, "c%d" % k: one.cross_p,
+                "s%d" % k: one.start, "g%d" % k: functools.partial(one.send_q, "xp", "xm"),
+                "u%d" % k: functools.partial(one.send_q, "x"), "t%d" % k: functools.partial(one.send_p, 0),
+                "v%d" % k: functools.partial(one.send_p, 1), "p%d" % k: functools.partial(one.pass_p, 0),
+                "P%d" % k: functools.partial(one.pass_p, 1), "f%d" % k: one.far_q, "n%d" % k: one.near_q,
+                "q%d" % k: one.pass_q, "c%d" % k: one.cross_p, "C%d" % k: one.keep_p,
                 "F%d" % k: functools.partial(one.finish, landing),
             })
             if gather is not None:
                 to = Gather(copies, w, k, gather)
                 table.update({
-                    "a%d" % k: functools.partial(to.first, one), "x%d" % k: to.across,
+                    "a%d" % k: functools.partial(to.first, one), "b%d" % k: functools.partial(to.first_q, one), "x%d" % k: to.across,
                     "k%d" % k: functools.partial(to.forward_p, 0), "r%d" % k: to.forward_q,
                     "l%d" % k: functools.partial(to.forward_p, 1), "z%d" % k: to.across_q, "e%d" % k: to.finish,
                 })

time: 135 us -> 130 us (0.963)
  Pallas kernels: 134 us -> 128 us
    pallas_call x1, Pallas kernels: 131 us -> 125 us  [epochs(): pl.pallas_call(epochs_kernel, out_shape=[jax.ShapeDtypeStruct(users.shape...]
where the time goes in v4:
time: 130 us; the launch traced here: 128 us
  Pallas kernels  128 us (98%)
    pallas_call x1, Pallas kernels, epochs(): pl.pallas_call(epochs_kernel, out_shape=[jax.ShapeDtypeStruct(users.shape...  125 us

profile of v4, /device:TPU:0, one launch (start us, length us, event | category | flops | bytes accessed | tf_op | source)
XLA Modules:
  0.0 128.4 jit_solution(2688931764993812872)
XLA Ops:
  0.6 125.4 %epochs.1 = (f32[2048,128]{1,0:T(8,128)}, f32[2048,128]{1,0:T(8,128)}) custom-call(s32[2]{0:T(128)} %bitcast.12, s32[2]{0:T(128)} %bitcast.13, s32[2,64]{1,0:T(2,128)} %bitcast.10, s32[2,64]{1,0:T(2,128)} %bitcast.11, bf16[2,64,256,256]{3,2,1,0:T(8,128)(2,1)} %bitcast.7, s32[2,64,256]{2,1,0:T(8,128)} %bitcast.9, f32[2048,128]{1,0:T(8,128)} %users_in.1, ...), custom_call_target="tpu_custom_call" | custom-call | tf_op jit(solution)/shard_map/epochs/pallas_call | solution.py:619
  126.0 2.4 %settle.1 = (f32[2048,128]{1,0:T(8,128)}, f32[2048,128]{1,0:T(8,128)}) custom-call(f32[2048,128]{1,0:T(8,128)} %get-tuple-element.4.a, f32[2048,128]{1,0:T(8,128)} %get-tuple-element.5.b), custom_call_target="tpu_custom_call" | custom-call | tf_op jit(solution)/shard_map/settle/pallas_call | solution.py:692

commit v5 on v4

--- a/solution.py
+++ b/solution.py
@@ -106,14 +106,15 @@
 COPIES = 160
 
 ORDER_0 = (
-    "s0", "g0", "t0", "B", "U", "p0", "s1", "c0", "P0", "v0", "U", "f0", "u0", "g1", "I", "n0",
-    "p1", "q0", "u1", "t1", "v1", "C0", "F0", "f1", "P1", "c1", "n1", "q1", "a0", "U", "b0", "C1",
-    "F1", "x0", "U", "a1", "r0", "b1", "x1", "z0", "V", "l0", "r1", "l1", "z1", "k0", "k1",
+    "s0", "g0", "t0", "B", "U", "p0", "s1", "P0", "c0", "v0", "U", "f0", "u0", "g1", "I", "n0",
+    "p1", "q0", "u1", "t1", "v1", "C0", "H0", "F0", "f1", "P1", "c1", "n1", "q1", "a0", "b0", "U",
+    "C1", "H1", "F1", "x0", "a1", "b1", "U", "r0", "x1", "z0", "G", "r1", "W", "l0", "l1", "z1",
+    "k0", "k1",
 )
 ORDER_1 = (
-    "s0", "g0", "B", "s1", "p0", "t0", "g1", "u0", "P0", "f0", "u1", "U", "t1", "U", "I", "c0",
-    "v1", "v0", "U", "n0", "p1", "U", "f1", "q0", "n1", "P1", "c1", "C0", "q1", "F0", "C1", "F1",
-    "V", "O",
+    "s0", "g0", "v0", "B", "s1", "t0", "U", "t1", "U", "p0", "g1", "G", "f0", "U", "n0", "p1",
+    "u0", "c0", "P0", "q0", "I", "P1", "f1", "c1", "v1", "U", "C0", "H0", "u1", "n1", "F0", "q1",
+    "C1", "F1", "H1", "W", "O",
 )
 
 
@@ -230,40 +231,42 @@
 
         in_steps(P_ROWS, 48, fn)
 
-    def finish(self, landing):
-        w, b, x, total = self.w, self.bufs, self.w["x"], self.total
+    def update(self, start, rows, grad, landing):
+        @pl.loop(0, rows // 32)
+        def _(k):
+            at = start // 32 + k
+            col = pl.multiple_of(lax.rem(at, 2) * 32, 32) + HALF * self.wave
+            old = self.base[lax.div(at, 2), pl.ds(col, 32), :]
+            new = (old - LEARN * grad(pl.multiple_of(k * 32, 32))).astype(BF16)
+            self.newv[at * 2] = new[:UNIT]
+            self.newv[at * 2 + 1] = new[UNIT:]
+
+        place, owner = landing
+        return self.c.start(
+            self.newv.at[units(0, start, rows)], place.at[self.wave].at[units(owner, start, rows)], self.w["to_next"]
+        )
+
+    def finish_q(self, landing):
+        b, x = self.bufs, self.w["x"]
         self.add_q(self.q["x"], x)
         for copy in self.q2:
             copy.wait_recv()
 
-        def fn(k):
-            s, t = pl.ds(k, 112), pl.ds(k + P_ROWS, 112)
+        def grad(k):
+            s = pl.ds(k, 32)
             both = b["q2p"][s, :].astype(F32) + b["q2m"][s, :].astype(F32)
-            total[t, :] = b["rq"][x, s, :].astype(F32) + both
-
-        in_steps(Q_ROWS, 112, fn)
+            return b["rq"][x, s, :].astype(F32) + both
+
+        self.shift_q = self.update(P_ROWS, Q_ROWS, grad, landing)
+
+    def finish_p(self, landing):
         self.y.wait_recv()
 
-        def fn(k):
-            s = pl.ds(k, 48)
-            total[s, :] = total[s, :] + b["ry"][s, :].astype(F32)
-
-        in_steps(P_ROWS, 48, fn)
-
-        @pl.loop(0, OWNERS)
-        def _(k):
-            s = pl.ds(pl.multiple_of(k * HALF, HALF), HALF)
-            old = self.base[k, pl.ds(HALF * self.wave, HALF), :]
-            new = (old - LEARN * total[s, :]).astype(BF16)
-            for u in range(TILE_UNITS):
-                self.newv[k * TILE_UNITS + u] = new[u * UNIT : (u + 1) * UNIT]
-
-        landing, owner = landing
-        landing = landing.at[self.wave]
-        self.shift = [
-            self.c.start(self.newv.at[units(0, at, n)], landing.at[units(owner, at, n)], w["to_next"])
-            for at, n in ((0, P_ROWS), (P_ROWS, Q_ROWS))
-        ]
+        def grad(k):
+            s = pl.ds(k, 32)
+            return self.total[s, :] + self.bufs["ry"][s, :].astype(F32)
+
+        self.shift_p = self.update(0, P_ROWS, grad, landing)
 
 
 class Gather:
@@ -275,16 +278,16 @@
         return self.c.start(ref, ref, self.w[to])
 
     def first(self, one):
-        shift, me = one.shift, self.w["g"]
+        me = self.w["g"]
         p = (0, P_ROWS)
-        shift[0].wait_recv()
+        one.shift_p.wait_recv()
         self.py = self.along(me, p, "to_y")
         self.pp = [self.along(me, p, "to_xp")]
         self.pm = [self.along(me, p, "to_xm")]
 
     def first_q(self, one):
         me, q = self.w["g"], (P_ROWS, Q_ROWS)
-        one.shift[1].wait_recv()
+        one.shift_q.wait_recv()
         self.qp = self.along(me, q, "to_xp")
         self.qm = self.along(me, q, "to_xm")
         self.rest = [self.along(me, q, "to_y")]
@@ -373,7 +376,6 @@
 
     arriving = [items_here(k) for k in range(stages)]
     mask_here = local_copy(mask_in, mask, 1)
-    own_here = local_copy(items_in.at[pl.ds(w["g"] * OWNERS, OWNERS)], vown, 2)
 
     def fetch(e, k):
         s = pl.ds(k * GROUP, GROUP)
@@ -488,6 +490,8 @@
 
     def item_base(e, copy):
         copy.wait_recv()
+        if e == 0:
+            own_here.wait()
         pull = (gsend[e, 2] + grecv[e, 2]).astype(F32)
 
         @pl.loop(0, OWNERS)
@@ -533,12 +537,13 @@
 
         if k + stages < OWNERS:
             arriving.append(items_here(k + stages))
-        for c in range(chunks // OWNERS * k, chunks // OWNERS * (k + 1)):
-            fetch(0, c).start()
+        for c in range(2 * (k - OWNERS // 2), 2 * (k - OWNERS // 2) + 2):
+            if c >= 0:
+                fetch(0, c).start()
     gram_copy = spread_gram(0, 1, gram_copy)
     mask_here.wait()
     lists_out.wait()
-    own_here.wait()
+    own_here = local_copy(items_in.at[pl.ds(w["g"] * OWNERS, OWNERS)], vown, 2)
 
     def steps(e, vt, landing, gather):
         waves = sums(e)
@@ -550,7 +555,7 @@
                 "v%d" % k: functools.partial(one.send_p, 1), "p%d" % k: functools.partial(one.pass_p, 0),
                 "P%d" % k: functools.partial(one.pass_p, 1), "f%d" % k: one.far_q, "n%d" % k: one.near_q,
                 "q%d" % k: one.pass_q, "c%d" % k: one.cross_p, "C%d" % k: one.keep_p,
-                "F%d" % k: functools.partial(one.finish, landing),
+                "F%d" % k: functools.partial(one.finish_p, landing), "H%d" % k: functools.partial(one.finish_q, landing),
             })
             if gather is not None:
                 to = Gather(copies, w, k, gather)
@@ -566,7 +571,9 @@
             done[0] += 2
 
         table.update(B=functools.partial(second_pass, e), U=some_users)
-        table["V"] = lambda: user_update(e, item_gram(vt))
+        pull = []
+        table["G"] = lambda: pull.append(item_gram(vt))
+        table["W"] = lambda: user_update(e, pull[0])
         return waves, table
 
     first_pass(0, vt0)
@@ -592,9 +599,9 @@
     for step in ORDER_1:
         table[step]()
     users_gone = sent[0]
-    s0, s1 = waves
-    for copy in s0.shift + s1.shift:
-        copy.wait_recv()
+    for one in waves:
+        one.shift_p.wait_recv()
+        one.shift_q.wait_recv()
 
     @pl.loop(0, OWNERS)
     def _(k):
@@ -645,7 +652,7 @@
             pltpu.VMEM((count, 3, RANK, RANK), BF16),
             pltpu.VMEM((count, 3, RANK, RANK), BF16),
             pltpu.VMEM((OWNERS, RANK, TILE), F32),
-            pltpu.VMEM((WAVES, WAVE_ROWS, TILE), F32),
+            pltpu.VMEM((WAVES, P_ROWS, TILE), F32),
             pltpu.VMEM((WAVES, WAVE_UNITS, UNIT, TILE), BF16),
             pltpu.VMEM((WAVES, WAVE_UNITS, UNIT, TILE), BF16),
             pltpu.VMEM(users.shape, F32),

time: 130 us -> 126 us (0.969); the launches traced: 128 us -> 126 us
  Pallas kernels: 128 us -> 125 us
    pallas_call x1, Pallas kernels: 125 us -> 123 us  [epochs(): pl.pallas_call(epochs_kernel, out_shape=[jax.ShapeDtypeStruct(users.shape...]
where the time goes in v5:
time: 126 us
  Pallas kernels  125 us (99%)
    pallas_call x1, Pallas kernels, epochs(): pl.pallas_call(epochs_kernel, out_shape=[jax.ShapeDtypeStruct(users.shape...  123 us

profile of v5, /device:TPU:0, one launch (start us, length us, event | category | flops | bytes accessed | tf_op | source)
XLA Modules:
  0.0 125.8 jit_solution(9590130077085389850)
XLA Ops:
  0.6 122.7 %epochs.1 = (f32[2048,128]{1,0:T(8,128)}, f32[2048,128]{1,0:T(8,128)}) custom-call(s32[2]{0:T(128)} %bitcast.12, s32[2]{0:T(128)} %bitcast.13, s32[2,64]{1,0:T(2,128)} %bitcast.10, s32[2,64]{1,0:T(2,128)} %bitcast.11, bf16[2,64,256,256]{3,2,1,0:T(8,128)(2,1)} %bitcast.7, s32[2,64,256]{2,1,0:T(8,128)} %bitcast.9, f32[2048,128]{1,0:T(8,128)} %users_in.1, ...), custom_call_target="tpu_custom_call" | custom-call | tf_op jit(solution)/shard_map/epochs/pallas_call | solution.py:626
  123.4 2.4 %settle.1 = (f32[2048,128]{1,0:T(8,128)}, f32[2048,128]{1,0:T(8,128)}) custom-call(f32[2048,128]{1,0:T(8,128)} %get-tuple-element.4.a, f32[2048,128]{1,0:T(8,128)} %get-tuple-element.5.b), custom_call_target="tpu_custom_call" | custom-call | tf_op jit(solution)/shard_map/settle/pallas_call | solution.py:699

commit v6 on v5

--- a/solution.py
+++ b/solution.py
@@ -510,21 +510,22 @@
         at = {k: v.at[e] for k, v in bufs.items()}
         return [Sum(copies, w, wave, part, at, base, total, newv) for wave in range(WAVES)]
 
-    for copy in lists_in:
-        copy.wait()
-    for e in range(ratings.shape[0]):
-        for k, keys in enumerate((cols_v, rows_v)):
-            prev, final_slot = chains(keys[e : e + 1, :], counts[e])
-            at = e * LISTS + k
-            lists[at : at + 1, 0:SLOTS] = prev
-            lists[at + 2 : at + 3, 0:SLOTS] = final_slot
-    lists_out = local_copy(lists, idx, 7)
-    users_here.wait()
-    gram_copy = prepare_users(0, True)
     zero = jnp.zeros((HALF, TILE), F32)
     acc[0, SLOTS] = zero
     acc[1, SLOTS] = zero
     for k in range(OWNERS):
+        if k == stages:
+            for copy in lists_in:
+                copy.wait()
+            for e in range(ratings.shape[0]):
+                for n, keys in enumerate((cols_v, rows_v)):
+                    prev, final_slot = chains(keys[e : e + 1, :], counts[e])
+                    at = e * LISTS + n
+                    lists[at : at + 1, 0:SLOTS] = prev
+                    lists[at + 2 : at + 3, 0:SLOTS] = final_slot
+            lists_out = local_copy(lists, idx, 7)
+            users_here.wait()
+            gram_copy = prepare_users(0, True)
         arriving[k].wait()
 
         @pl.loop(0, OWNERS, unroll=2)

time: 126 us -> 127 us (level)
  no operation moved by 1% of the time
where the time goes in v6:
time: 127 us
  Pallas kernels  126 us (99%)
    pallas_call x1, Pallas kernels, epochs(): pl.pallas_call(epochs_kernel, out_shape=[jax.ShapeDtypeStruct(users.shape...  123 us

profile of v6, /device:TPU:0, one launch (start us, length us, event | category | flops | bytes accessed | tf_op | source)
XLA Modules:
  0.0 126.5 jit_solution(17828930885980558990)
XLA Ops:
  0.6 123.5 %epochs.1 = (f32[2048,128]{1,0:T(8,128)}, f32[2048,128]{1,0:T(8,128)}) custom-call(s32[2]{0:T(128)} %bitcast.12, s32[2]{0:T(128)} %bitcast.13, s32[2,64]{1,0:T(2,128)} %bitcast.10, s32[2,64]{1,0:T(2,128)} %bitcast.11, bf16[2,64,256,256]{3,2,1,0:T(8,128)(2,1)} %bitcast.7, s32[2,64,256]{2,1,0:T(8,128)} %bitcast.9, f32[2048,128]{1,0:T(8,128)} %users_in.1, ...), custom_call_target="tpu_custom_call" | custom-call | tf_op jit(solution)/shard_map/epochs/pallas_call | solution.py:627
  124.1 2.4 %settle.1 = (f32[2048,128]{1,0:T(8,128)}, f32[2048,128]{1,0:T(8,128)}) custom-call(f32[2048,128]{1,0:T(8,128)} %get-tuple-element.4.a, f32[2048,128]{1,0:T(8,128)} %get-tuple-element.5.b), custom_call_target="tpu_custom_call" | custom-call | tf_op jit(solution)/shard_map/settle/pallas_call | solution.py:700
